TPU v7x, 32 devices: a whole 2x2x4 slice. The times are simulated.
32 devices in a mesh: batch: 4 (over y, x), seq: 4 (over z), head: 2 (over core).
Axes of the slice: x: 2, y: 2, z: 4, core: 2. Of those that a mesh axis runs over, the one named last changes fastest.
Arguments:
- hidden: bfloat16 [8, 4096, 1024], P('batch', 'seq', 'head'), may hold values from -6 to 6
- cotangent: bfloat16 [8, 4096, 1024], P('batch', 'seq', 'head'), may hold values from -6 to 6
- norm_gain: bfloat16 [1024], P('head'), may hold values from 0.099609375 to 1.8984375
- proj_gate: bfloat16 [1024, 2048], P(None, 'head'), may hold values from -0.1875 to 0.1875
- proj_values: bfloat16 [1024, 2048], P(None, 'head'), may hold values from -0.1875 to 0.1875
- proj_state: bfloat16 [1024, 256], P(None, 'head'), may hold values from -0.1875 to 0.1875
- proj_steps: bfloat16 [1024, 32], P(None, 'head'), may hold values from -0.1875 to 0.1875
- conv_values: float32 [4, 2048], P(None, 'head'), may hold values from -3 to 3
- conv_state: float32 [4, 256], P(None, 'head'), may hold values from -3 to 3
- bias_values: float32 [2048], P('head'), may hold values from -2 to 2
- bias_state: float32 [256], P('head'), may hold values from -2 to 2
- step_bias: float32 [32], P('head'), may hold values from -6 to -1
- log_rates: float32 [32], P('head'), may hold values from -3 to 1
- skip_gain: float32 [32], P('head'), may hold values from 0.5 to 1.5
- gate_gain: float32 [2048], P('head'), may hold values from 0.1 to 1.9
- proj_output: bfloat16 [2048, 1024], P('head'), may hold values from -0.125 to 0.125
Outputs:
- block_out: bfloat16 [8, 4096, 1024], P('batch', 'seq', 'head')
- grad_hidden: float32 [8, 4096, 1024], P('batch', 'seq', 'head')
- grad_norm_gain: float32 [1024], P('head')
- grad_proj_gate: float32 [1024, 2048], P(None, 'head')
- grad_proj_values: float32 [1024, 2048], P(None, 'head')
- grad_proj_state: float32 [1024, 256], P(None, 'head')
- grad_proj_steps: float32 [1024, 32], P(None, 'head')
- grad_conv_values: float32 [4, 2048], P(None, 'head')
- grad_conv_state: float32 [4, 256], P(None, 'head')
- grad_bias_values: float32 [2048], P('head')
- grad_bias_state: float32 [256], P('head')
- grad_step_bias: float32 [32], P('head')
- grad_log_rates: float32 [32], P('head')
- grad_skip_gain: float32 [32], P('head')
- grad_gate_gain: float32 [2048], P('head')
- grad_proj_output: float32 [2048, 1024], P('head')
All inputs are finite; a program needn't handle non-finite values.
Results may differ from a plain program's by a relative error of at most 0.0093.
Values may be sent and summed in bfloat16 or wider, within the bound.
A program may use at most 512 MiB of HBM per device.

v0:
```python
import jax
import jax.numpy as jnp
from jax import lax
from jax.sharding import PartitionSpec as P

SPAN = 256


epsilon = 1e-05
highest = lax.Precision.HIGHEST


def from_behind(block, axis, distance):
    devices = range(lax.axis_size(axis))
    route = [(i - distance, i) for i in devices if i - distance in devices]
    return lax.ppermute(block, axis, route)


def entering_2(array, axis, combine, identity, reverse):
    length, index = (lax.axis_size(axis), lax.axis_index(axis))
    everything = jax.tree.map(lambda part: lax.all_gather(part, axis), array)
    start = jax.tree.map(
        lambda part, zero: jnp.broadcast_to(jnp.asarray(zero, part.dtype), part.shape),
        array,
        identity,
    )

    def step(k, before):
        at = length - 1 - k if reverse else k
        reached = at > index if reverse else at < index
        new = combine(before, jax.tree.map(lambda part: part[at], everything))
        return jax.tree.map(lambda a, b: jnp.where(reached, a, b), new, before)

    return lax.fori_loop(0, length, step, start)


def silu_slope(value):
    logistic = jax.nn.sigmoid(value)
    return logistic * (1.0 + value * (1.0 - logistic))


def relay(earlier, later):
    return (earlier[0] + later[0], earlier[1] * jnp.exp(later[0])[:, :, None, None] + later[1])


def convolve(signal, edges, kernel, offset):
    padded = jnp.concatenate([edges, signal], axis=1)
    length = signal.shape[1]
    result = offset + kernel[0] * padded[:, 0:length]
    for position in range(1, kernel.shape[0]):
        result = result + kernel[position] * padded[:, position : position + length]
    return result


def span_scan(values, steps, rates, writes, readout):
    groups, length, heads_here, headdim = values.shape
    blocks = length // SPAN
    causal = jnp.tril(jnp.ones((SPAN, SPAN), dtype=bool))[None, :, :, None]

    def by_block(array):
        shaped = array.reshape((groups, blocks, SPAN) + array.shape[2:])
        return jnp.moveaxis(shaped, 1, 0)

    def span_step(state, block):
        block_values, block_steps, block_writes, block_reads = block
        cumul = jnp.cumsum(block_steps * rates, axis=1)
        scores = jnp.einsum("stn,sun->stu", block_reads, block_writes, precision=highest)
        differ = cumul[:, :, None, :] - cumul[:, None, :, :]
        decays = jnp.where(causal, jnp.exp(jnp.where(causal, differ, 0.0)), 0.0)
        mixing = decays * scores[:, :, :, None] * block_steps[:, None, :, :]
        inner = jnp.einsum("stuh,suhp->sthp", mixing, block_values, precision=highest)
        carried = (
            jnp.einsum("stn,shpn->sthp", block_reads, state, precision=highest)
            * jnp.exp(cumul)[:, :, :, None]
        )
        total = cumul[:, -1]
        tail = jnp.exp(total[:, None, :] - cumul) * block_steps
        fresh = jnp.einsum(
            "suh,suhp,sun->shpn", tail, block_values, block_writes, precision=highest
        )
        return (state * jnp.exp(total)[:, :, None, None] + fresh, inner + carried)

    start = jnp.zeros((groups, heads_here, headdim, writes.shape[2]), jnp.float32)
    final_state, outputs = lax.scan(
        span_step, start, (by_block(values), by_block(steps), by_block(writes), by_block(readout))
    )
    return (jnp.moveaxis(outputs, 0, 1).reshape(values.shape), final_state)


def local_ssd(values, dt_raw, step_bias, log_rates, writes, readout, entering):
    steps = jax.nn.softplus(dt_raw + step_bias)
    rates = -jnp.exp(log_rates)
    zero_out, zero_final = span_scan(values, steps, rates, writes, readout)
    cumseg = jnp.cumsum(steps * rates, axis=1)
    carried = (
        jnp.einsum("sln,shpn->slhp", readout, entering, precision=highest)
        * jnp.exp(cumseg)[:, :, :, None]
    )
    ending = zero_final + jnp.exp(cumseg[:, -1])[:, :, None, None] * entering
    return (zero_out + carried, ending)


def per_device(
    hidden,
    cotangent,
    norm_gain,
    proj_gate,
    proj_values,
    proj_state,
    proj_steps,
    conv_values,
    conv_state,
    bias_values,
    bias_state,
    step_bias,
    log_rates,
    skip_gain,
    gate_gain,
    proj_output,
):
    groups, length, width_share = hidden.shape
    tokens = groups * length
    whole_rows, gain_whole = (
        lax.all_gather(hidden, "head", axis=2, tiled=True),
        lax.all_gather(norm_gain, "head", axis=0, tiled=True),
    )
    inputs = whole_rows.astype(jnp.float32).reshape(tokens, -1)
    width_full = inputs.shape[1]
    gain_float = gain_whole.astype(jnp.float32)
    inv_rms = lax.rsqrt(jnp.mean(inputs * inputs, axis=1, keepdims=True) + epsilon)
    unit_rows = inputs * inv_rms
    normed = (unit_rows * gain_float).astype(jnp.bfloat16)
    gate_pre = jnp.dot(normed, proj_gate, preferred_element_type=jnp.float32)
    value_pre = jnp.dot(normed, proj_values, preferred_element_type=jnp.float32)
    state_pre = jnp.dot(normed, proj_state, preferred_element_type=jnp.float32)
    steps_pre = jnp.dot(normed, proj_steps, preferred_element_type=jnp.float32)
    inner_share = value_pre.shape[1]
    heads_here = steps_pre.shape[1]
    headdim = inner_share // heads_here
    mixed_pre = jnp.concatenate([value_pre, state_pre], axis=1).reshape(groups, length, -1)
    kernel = jnp.concatenate([conv_values, conv_state], axis=1)
    offset = jnp.concatenate([bias_values, bias_state])
    margin = kernel.shape[0] - 1
    edges = from_behind(mixed_pre[:, length - margin :], "seq", 1)
    conv_pre = convolve(mixed_pre, edges, kernel, offset)
    activated = jax.nn.silu(conv_pre)
    values = activated[:, :, :inner_share].reshape(groups, length, heads_here, headdim)
    maps_full = lax.all_gather(activated[:, :, inner_share:], "head", axis=2, tiled=True)
    state_size = maps_full.shape[2] // 2
    writes = maps_full[:, :, :state_size]
    readout = maps_full[:, :, state_size:]
    dt_raw = steps_pre.reshape(groups, length, heads_here)
    steps = jax.nn.softplus(dt_raw + step_bias)
    rates = -jnp.exp(log_rates)
    zero_out, zero_final = span_scan(values, steps, rates, writes, readout)
    cumseg = jnp.cumsum(steps * rates, axis=1)
    total_log = cumseg[:, -1]
    identity = (jnp.zeros_like(total_log), jnp.zeros_like(zero_final))
    entering = entering_2((total_log, zero_final), "seq", relay, identity, False)[1]
    carried = (
        jnp.einsum("sln,shpn->slhp", readout, entering, precision=highest)
        * jnp.exp(cumseg)[:, :, :, None]
    )
    core = (zero_out + carried + skip_gain[:, None] * values).reshape(tokens, inner_share)
    gate_act = jax.nn.silu(gate_pre)
    gated = core * gate_act
    square_sum = lax.psum(jnp.sum(gated * gated, axis=1), "head")
    inner_full = inner_share * lax.axis_size("head")
    inv_gate = lax.rsqrt(square_sum / inner_full + epsilon)[:, None]
    gate_unit = gated * inv_gate
    gate_normed = (gate_unit * gate_gain).astype(jnp.bfloat16)
    out_terms = jnp.dot(gate_normed, proj_output, preferred_element_type=jnp.float32)
    out_share = lax.psum_scatter(
        out_terms.reshape(groups, length, width_full), "head", scatter_dimension=2, tiled=True
    )
    block_out = (hidden.astype(jnp.float32) + out_share).astype(jnp.bfloat16)
    cot_whole = lax.all_gather(cotangent, "head", axis=2, tiled=True).reshape(tokens, width_full)
    grad_proj_output = jnp.dot(gate_normed.T, cot_whole, preferred_element_type=jnp.float32)
    back_gnorm = jnp.dot(cot_whole, proj_output.T, preferred_element_type=jnp.float32)
    grad_gate_gain = jnp.sum(back_gnorm * gate_unit, axis=0)
    scaled_gate = back_gnorm * gate_gain
    gate_inner = lax.psum(jnp.sum(scaled_gate * gate_unit, axis=1), "head")
    back_gated = inv_gate * (scaled_gate - gate_unit * (gate_inner / inner_full)[:, None])
    back_core = (back_gated * gate_act).reshape(groups, length, heads_here, headdim)
    back_gate = (back_gated * core * silu_slope(gate_pre)).astype(jnp.bfloat16)
    grad_skip_gain = jnp.sum(back_core * values, axis=(0, 1, 3))
    entry_grad = jnp.einsum(
        "slhp,sln->shpn", back_core * jnp.exp(cumseg)[:, :, :, None], readout, precision=highest
    )
    later_grad = entering_2((total_log, entry_grad), "seq", relay, identity, True)[1]
    primal_ssd, ssd_pull = jax.vjp(
        local_ssd, values, dt_raw, step_bias, log_rates, writes, readout, entering
    )
    (
        back_values,
        back_dt,
        grad_step_bias,
        grad_log_rates,
        back_writes,
        back_readout,
        unused_entry,
    ) = ssd_pull((back_core, later_grad))
    back_values = back_values + skip_gain[:, None] * back_core
    back_maps = lax.psum_scatter(
        jnp.concatenate([back_writes, back_readout], axis=2),
        "head",
        scatter_dimension=2,
        tiled=True,
    )
    back_act = jnp.concatenate(
        [back_values.reshape(groups, length, inner_share), back_maps], axis=2
    )
    back_conv = back_act * silu_slope(conv_pre)
    primal_conv, conv_pull = jax.vjp(convolve, mixed_pre, edges, kernel, offset)
    back_mixed, back_edges, grad_kernel, grad_offset = conv_pull(back_conv)
    returned = from_behind(back_edges, "seq", -1)
    back_mixed = back_mixed + jnp.pad(returned, ((0, 0), (length - margin, 0), (0, 0)))
    back_mixed = back_mixed.reshape(tokens, -1).astype(jnp.bfloat16)
    back_value_pre = back_mixed[:, :inner_share]
    back_state_pre = back_mixed[:, inner_share:]
    back_steps_pre = back_dt.reshape(tokens, heads_here).astype(jnp.bfloat16)
    grad_proj_gate = jnp.dot(normed.T, back_gate, preferred_element_type=jnp.float32)
    grad_proj_values = jnp.dot(normed.T, back_value_pre, preferred_element_type=jnp.float32)
    grad_proj_state = jnp.dot(normed.T, back_state_pre, preferred_element_type=jnp.float32)
    grad_proj_steps = jnp.dot(normed.T, back_steps_pre, preferred_element_type=jnp.float32)
    back_normed = jnp.dot(back_gate, proj_gate.T, preferred_element_type=jnp.float32)
    back_normed = back_normed + jnp.dot(
        back_value_pre, proj_values.T, preferred_element_type=jnp.float32
    )
    back_normed = back_normed + jnp.dot(
        back_state_pre, proj_state.T, preferred_element_type=jnp.float32
    )
    back_normed = back_normed + jnp.dot(
        back_steps_pre, proj_steps.T, preferred_element_type=jnp.float32
    )
    first_column = lax.axis_index("head") * width_share
    normed_total = lax.psum(back_normed, "head")
    scaled_input = normed_total * gain_float
    input_inner = jnp.sum(scaled_input * unit_rows, axis=1, keepdims=True) / width_full
    back_input = inv_rms * (scaled_input - unit_rows * input_inner)
    back_input = lax.dynamic_slice_in_dim(back_input, first_column, width_share, 1)
    gain_grad_full = jnp.sum(normed_total * unit_rows, axis=0)
    grad_norm_gain = lax.dynamic_slice_in_dim(gain_grad_full, first_column, width_share, 0)
    grad_hidden = cotangent.astype(jnp.float32) + back_input.reshape(groups, length, width_share)
    summed = lax.psum(
        (
            grad_norm_gain,
            grad_proj_gate,
            grad_proj_values,
            grad_proj_state,
            grad_proj_steps,
            grad_kernel[:, :inner_share],
            grad_kernel[:, inner_share:],
            grad_offset[:inner_share],
            grad_offset[inner_share:],
            grad_step_bias,
            grad_log_rates,
            grad_skip_gain,
            grad_gate_gain,
            grad_proj_output,
        ),
        ("batch", "seq"),
    )
    return (
        block_out,
        grad_hidden,
        summed[0],
        summed[1],
        summed[2],
        summed[3],
        summed[4],
        summed[5],
        summed[6],
        summed[7],
        summed[8],
        summed[9],
        summed[10],
        summed[11],
        summed[12],
        summed[13],
    )


def solution(mesh):
    in_specs = (
        P("batch", "seq", "head"),
        P("batch", "seq", "head"),
        P("head"),
        P(None, "head"),
        P(None, "head"),
        P(None, "head"),
        P(None, "head"),
        P(None, "head"),
        P(None, "head"),
        P("head"),
        P("head"),
        P("head"),
        P("head"),
        P("head"),
        P("head"),
        P("head", None),
    )
    out_specs = (
        P("batch", "seq", "head"),
        P("batch", "seq", "head"),
        P("head"),
        P(None, "head"),
        P(None, "head"),
        P(None, "head"),
        P(None, "head"),
        P(None, "head"),
        P(None, "head"),
        P("head"),
        P("head"),
        P("head"),
        P("head"),
        P("head"),
        P("head"),
        P("head", None),
    )
    return jax.shard_map(
        per_device, mesh=mesh, in_specs=in_specs, out_specs=out_specs, check_vma=False
    )
```

profile of v0, /device:TPU:0, one launch (start us, length us, event | category | flops | bytes accessed | tf_op | source)
XLA Modules:
  0.0 1842.8 jit_solution(18088021706908163592)
XLA Ops:
  12.1 13.9 all-gather.10.cloned.1.call-done
  67.4 18.1 fusion.142
  142.3 96.6 %while.117 = (s32[]{:T(128)}, f32[2,16,64,128]{3,2,1,0:T(8,128)S(1)}, f32[4,2,256,16,64]{2,4,3,1,0:T(8,128)}, f32[4,2,256,16]{2,3,1,0:T(8,128)S(1)}, f32[16]{0:T...) while((s32[]{:T(128)}, ...), condition=%wide.region_4.5_spmd.clone.clone, body=%wide.region_1.4_spmd.clone.clone.sunk | while | flops 3436806144 | bytes 16456260 | solution.py:84
  145.6 12.0 fusion.283
  169.8 12.0 fusion.283
  193.9 12.0 fusion.283
  217.9 12.0 fusion.283
  255.7 12.2 all-gather
  277.4 45.1 %all-gather.16.cloned.1.call-done = f32[8,16,64,128]{3,2,1,0:T(8,128)} async-done(((f32[2,16,64,128]{3,2,1,0:T(8,128)}), f32[8,16,64,128]{3,2,1,0:T(8,128)}) %all-gather.16.cloned.1.call-update) | async-done | bytes 4194320 | tf_op jit(solution)/shard_map/all_gather | solution.py:21
  322.5 11.1 while.115
  353.3 14.5 copy.364
  367.9 14.5 reshape.548
  382.4 13.5 multiply_reduce_fusion.9
  398.4 14.8 multiply_reduce_fusion.4
  415.6 20.9 %fusion.143 = (f32[1024]{0:T(1024)}, f32[2048,1024]{1,0:T(8,128)}, bf16[2048,1024]{1,0:T(8,128)(2,1)}) fusion(f32[2,1024,1024]{2,1,0:T(8,128)} %slice.181, f32[2048,1024]{1,0:T(8,128)} %get-tuple-element.2138, f32[2048]{0:T(1024)S(1)} %broadcast_multiply_fusion.6, f32[2048,1024]{1,0:T(8,128)} %get-tuple-element.2100, f32[2048,1024]{1,0:T(8,128)} %get-tuple-element.2139, ...), kind=kLoop, calls=%fused_computation.225 | loop fusion | flops 39844864 | bytes 54550528 | tf_op jit(solution)/shard_map/reduce_sum | solution.py:186
  445.6 11.7 reshape.500
  457.3 13.8 fusion.146
  480.2 130.9 %while.118 = (s32[]{:T(128)}, f32[2,16,64,128]{3,2,1,0:T(8,128)S(1)}, f32[4,2,256,256,16]{3,4,2,1,0:T(8,128)}, f32[4,2,256,256,1]{3,2,1,4,0:T(8,128)}, f32[4,2,2...) while((s32[]{:T(128)}, ...), condition=%wide.region_19.20_spmd.clone.clone, body=%wide.region_16.19_spmd.clone.clone.sunk | while | flops 1825874048 | bytes 51787120 | solution.py:84
  484.4 13.2 multiply_dynamic-update-slice_fusion.2
  517.2 13.2 multiply_dynamic-update-slice_fusion.2
  549.9 13.2 multiply_dynamic-update-slice_fusion.2
  582.5 13.2 multiply_dynamic-update-slice_fusion.2
  611.1 10.9 reshape_reshape.8
  640.8 534.2 %while.119 = (s32[]{:T(128)}, f32[16]{0:T(128)S(1)}, f32[2,16,64,128]{3,2,1,0:T(8,128)S(1)}, f32[4,2,256,16,64]{2,4,3,1,0:T(8,128)}, f32[4,2,256,16]{3,1,2,0:T(2...) while((s32[]{:T(128)}, f32[16]{0:T(128)S(1)}, ...), condition=%wide.region_31.32_spmd.clone.clone, body=%wide.region_20.31_spmd.clone.clone.sunk | while | flops 6874554368 | bytes 176955184 | solution.py:84
  657.2 11.0 constant_dynamic-slice_fusion.16
  670.0 30.5 %fusion.299 = (f32[2,256,16]{1,2,0:T(8,128)}, f32[2,256,16]{1,2,0:T(8,128)S(1)}, f32[2,256,256]{2,1,0:T(8,128)}, f32[2,256,16]{1,2,0:T(8,128)}) fusion(f32[1,2,256,256,16]{3,4,2,1,0:T(8,128)S(1)} %get-tuple-element.2623, f32[2,256,256]{2,1,0:T(8,128)S(1)} %dynamic-slice_bitcast_fusion.12, f32[2,256,16]{1,2,0:T(8,128)S(1)} %dynamic-slice_bitcast_fusion.13, ...), kind=kOutput, calls=%fused_computation.156.clone.1 | convolution fusion | flops 1633525760 | bytes 30605316 | tf_op jit(solution)/shard_map/transpose(jvp())/while/body/eval_jaxpr/stuh,suhp->sthp/dot_general | solution.py:71
  748.9 14.5 bitcast_dynamic-update-slice_fusion.30
  782.8 11.0 constant_dynamic-slice_fusion.16
  795.6 41.9 %fusion.299 = (f32[2,256,16]{1,2,0:T(8,128)}, f32[2,256,16]{1,2,0:T(8,128)S(1)}, f32[2,256,256]{2,1,0:T(8,128)}, f32[2,256,16]{1,2,0:T(8,128)}) fusion(f32[1,2,256,256,16]{3,4,2,1,0:T(8,128)S(1)} %get-tuple-element.2623, f32[2,256,256]{2,1,0:T(8,128)S(1)} %dynamic-slice_bitcast_fusion.12, f32[2,256,16]{1,2,0:T(8,128)S(1)} %dynamic-slice_bitcast_fusion.13, ...), kind=kOutput, calls=%fused_computation.156.clone.1 | convolution fusion | flops 1633525760 | bytes 30605316 | tf_op jit(solution)/shard_map/transpose(jvp())/while/body/eval_jaxpr/stuh,suhp->sthp/dot_general | solution.py:71
  886.0 14.5 bitcast_dynamic-update-slice_fusion.30
  920.0 11.0 constant_dynamic-slice_fusion.16
  932.8 30.5 %fusion.299 = (f32[2,256,16]{1,2,0:T(8,128)}, f32[2,256,16]{1,2,0:T(8,128)S(1)}, f32[2,256,256]{2,1,0:T(8,128)}, f32[2,256,16]{1,2,0:T(8,128)}) fusion(f32[1,2,256,256,16]{3,4,2,1,0:T(8,128)S(1)} %get-tuple-element.2623, f32[2,256,256]{2,1,0:T(8,128)S(1)} %dynamic-slice_bitcast_fusion.12, f32[2,256,16]{1,2,0:T(8,128)S(1)} %dynamic-slice_bitcast_fusion.13, ...), kind=kOutput, calls=%fused_computation.156.clone.1 | convolution fusion | flops 1633525760 | bytes 30605316 | tf_op jit(solution)/shard_map/transpose(jvp())/while/body/eval_jaxpr/stuh,suhp->sthp/dot_general | solution.py:71
  1011.7 14.6 bitcast_dynamic-update-slice_fusion.30
  1045.6 11.0 constant_dynamic-slice_fusion.16
  1058.5 41.9 %fusion.299 = (f32[2,256,16]{1,2,0:T(8,128)}, f32[2,256,16]{1,2,0:T(8,128)S(1)}, f32[2,256,256]{2,1,0:T(8,128)}, f32[2,256,16]{1,2,0:T(8,128)}) fusion(f32[1,2,256,256,16]{3,4,2,1,0:T(8,128)S(1)} %get-tuple-element.2623, f32[2,256,256]{2,1,0:T(8,128)S(1)} %dynamic-slice_bitcast_fusion.12, f32[2,256,16]{1,2,0:T(8,128)S(1)} %dynamic-slice_bitcast_fusion.13, ...), kind=kOutput, calls=%fused_computation.156.clone.1 | convolution fusion | flops 1633525760 | bytes 30605316 | tf_op jit(solution)/shard_map/transpose(jvp())/while/body/eval_jaxpr/stuh,suhp->sthp/dot_general | solution.py:71
  1148.8 14.6 bitcast_dynamic-update-slice_fusion.30
  1176.4 17.0 fusion.159
  1195.1 11.9 fusion.187
  1228.6 14.5 copy.358
  1243.1 14.6 reshape.547
  1262.5 39.6 %reduce-window.68 = f32[2,16,8,128]{3,2,1,0:T(8,128)S(1)} reduce-window(f32[2,16,8,128]{3,2,1,0:T(8,128)S(1)} %copy.335, f32[]{:T(128)} %constant.269.clone.1), window={size=1x1x1x128 pad=0_0x0_0x0_0x0_127}, to_apply=%region_35.36 | reduce-window | flops 4161536 | bytes 262148 | tf_op jit(solution)/shard_map/reduce-window.4
  1308.8 12.1 multiply_add_fusion.1
  1320.9 26.1 %multiply_reduce_fusion.2 = (f32[1152]{0:T(1024)S(1)}, f32[1152]{0:T(1024)S(1)}, f32[1152]{0:T(1024)S(1)}, f32[1152]{0:T(1024)S(1)}, f32[1152]{0:T(1024)S(1)}, /*index=5*/f32[2,1024,1152]{2,1,0:T(8,128)}) fusion(f32[2,1024,1152]{2,1,0:T(8,128)} %bitcast.665, f32[2,3,1152]{2,1,0:T(4,128)S(1)} %copy-done.30, f32[2048,1152]{1,0:T(8,128)} %copy.363, ...), kind=kLoop, calls=%fused_computation.219 | loop fusion | flops 49539456 | bytes 47236608 | tf_op jit(solution)/shard_map/transpose(jvp())/reduce_sum | solution.py:51
  1359.7 12.2 pad_add_fusion
  1398.5 10.9 fusion.199
  1409.4 11.3 fusion.186
  1445.4 82.1 %all-reduce.11 = (f32[512]{0:T(512)}, f32[4,1024]{1,0:T(4,128)}, f32[4,128]{1,0:T(4,128)}, f32[1024]{0:T(1024)}, f32[128]{0:T(128)}, /*index=5*/f32[16]{0:T(128)}, f32[16]{0:T(128)}, f32[16]{0:T(128)}, f32[1024]{0:T(1024)}) all-reduce(f32[512]{0:T(512)S(1)} %dynamic_slice.287, ...), channel_id=1, replica_groups=mesh['batch'=4,'seq'=4,'head'=2] {'batch','seq'}, use_global_device_ids=true, to_apply=%region_40.41 | all-reduce | flops 7344 | bytes 58752 | tf_op jit(solution)/shard_map/psum | solution.py:245
  1534.9 290.7 %all-reduce.18.cloned.1.call-done = (f32[1024,1024]{1,0:T(8,128)}, f32[1024,1024]{1,0:T(8,128)}, f32[1024,128]{1,0:T(8,128)}, f32[1024,16]{0,1:T(8,128)}, f32[1024,1024]{1,0:T(8,128)}) async-done(((f32[1024,1024]{1,0:T(8,128)}, f32[1024,1024]{1,0:T(8,128)}, f32[1024,128]{1,0:T(8,128)}, f32[1024,16]{0,1:T(8,128)}, f32[1024,1024]{1,0:T(8,128)}), (f32[1024,1024]{1,0:T(8,128)}, f32[1024,1024]{1,0:T(8,128)}, ...) | async-done | bytes 13172752 | tf_op jit(solution)/shard_map/psum | solution.py:245
  (668 shorter events, 730.8 us)
Async XLA Ops:
  7.2 375.2 %copy-start = (bf16[1024,1024]{1,0:T(8,128)(2,1)S(1)}, bf16[1024,1024]{1,0:T(8,128)(2,1)}, u32[]{:S(2)}) copy-start(bf16[1024,1024]{1,0:T(8,128)(2,1)} %param.29) | copy-start | bytes 6291460
  7.2 18.8 %all-gather.10.cloned.1.call-start = ((), (), s32[]{:S(2)}) async-start(), calls=%async_computation.2 | async-start | bytes 6291456 | tf_op jit(solution)/shard_map/all_gather | solution.py:124
  7.9 126.8 %all-gather.12.cloned.1.call-start = ((), (), s32[]{:S(2)}) async-start(), calls=%async_computation.3 | async-start | bytes 3145728 | tf_op jit(solution)/shard_map/all_gather | solution.py:148
  10.6 80.7 %copy-start.47 = (f32[2,1,512]{2,1,0:T(1,128)}, f32[2,1,512]{2,1,0:T(1,128)S(1)}, u32[]{:S(2)}) copy-start(f32[2,1,512]{2,1,0:T(1,128)S(1)} %convert_element_type.56) | copy-start | bytes 12292
  12.0 55.3 %copy-start.33 = (f32[1152]{0:T(1024)}, f32[1152]{0:T(1024)S(1)}, u32[]{:S(2)}) copy-start(f32[1152]{0:T(1024)S(1)} %get-tuple-element.1927) | copy-start | bytes 13828
  12.1 55.3 %copy-start.35 = (f32[1152]{0:T(1024)}, f32[1152]{0:T(1024)S(1)}, u32[]{:S(2)}) copy-start(f32[1152]{0:T(1024)S(1)} %get-tuple-element.1928) | copy-start | bytes 13828
  12.1 55.3 %copy-start.37 = (f32[1152]{0:T(1024)}, f32[1152]{0:T(1024)S(1)}, u32[]{:S(2)}) copy-start(f32[1152]{0:T(1024)S(1)} %get-tuple-element.1929) | copy-start | bytes 13828
  12.1 55.3 %copy-start.39 = (f32[1152]{0:T(1024)}, f32[1152]{0:T(1024)S(1)}, u32[]{:S(2)}) copy-start(f32[1152]{0:T(1024)S(1)} %get-tuple-element.1930) | copy-start | bytes 13828
  29.1 62.2 %copy-start.60 = (f32[2,1024]{1,0:T(2,128)}, f32[2,1024]{1,0:T(2,128)S(1)}, u32[]{:S(2)}) copy-start(f32[2,1024]{1,0:T(2,128)S(1)} %get-tuple-element.2133) | copy-start | bytes 24580
  62.1 5.3 collective-permute-start
  67.3 18.2 copy-start.29
  67.4 23.3 %copy-start.69 = (f32[16]{0:T(128)S(1)}, f32[16]{0:T(128)}, u32[]{:S(2)}) copy-start(f32[16]{0:T(128)} %param.38) | copy-start | bytes 196
  67.4 23.9 %copy-start.49 = (bf16[1024,16]{0,1:T(8,128)(2,1)S(1)}, bf16[1024,16]{0,1:T(8,128)(2,1)}, u32[]{:S(2)}) copy-start(bf16[1024,16]{0,1:T(8,128)(2,1)} %param.32) | copy-start | bytes 98308
  67.4 23.9 %copy-start.73 = (f32[16]{0:T(128)S(1)}, f32[16]{0:T(128)}, u32[]{:S(2)}) copy-start(f32[16]{0:T(128)} %param.37) | copy-start | bytes 196
  90.2 232.4 %all-gather.16.cloned.1.call-start = ((), (), s32[]{:S(2)}) async-start(), calls=%async_computation.8 | async-start | bytes 5242880 | tf_op jit(solution)/shard_map/all_gather | solution.py:21
  95.4 145.9 %copy-start.24 = (f32[2,1024,16]{1,2,0:T(8,128)}, f32[2,1024,16]{1,2,0:T(8,128)S(1)}, u32[]{:S(2)}) copy-start(f32[2,1024,16]{1,2,0:T(8,128)S(1)} %get-tuple-element.2137) | copy-start | bytes 393220
  239.9 158.4 %all-gather.14.cloned.1.call-start = ((), (), s32[]{:S(2)}) async-start(), calls=%async_computation.5 | async-start | bytes 6291456 | tf_op jit(solution)/shard_map/all_gather | solution.py:177
  240.5 381.5 %all-gather.18.cloned.1.call-start = ((), (), s32[]{:S(2)}) async-start(), calls=%async_computation.9 | async-start | bytes 5242880 | tf_op jit(solution)/shard_map/all_gather | solution.py:21
  269.4 187.9 %copy-start.23 = (f32[2,1024,16]{1,2,0:T(8,128)}, f32[2,1024,16]{1,2,0:T(8,128)S(1)}, u32[]{:S(2)}) copy-start(f32[2,1024,16]{1,2,0:T(8,128)S(1)} %copy.307) | copy-start | bytes 393220
  333.7 19.7 %copy-start.46 = (f32[4,2,16]{2,1,0:T(2,128)}, f32[4,2,16]{2,1,0:T(2,128)S(1)}, u32[]{:S(2)}) copy-start(f32[4,2,16]{2,1,0:T(2,128)S(1)} %get-tuple-element.2975) | copy-start | bytes 1540
  398.3 17.3 copy-start.51
  471.1 849.7 %reduce-scatter.5.cloned.1.call-start = ((), (), s32[]{:S(2)}) async-start(), calls=%async_computation.6 | async-start | bytes 3145728 | tf_op jit(solution)/shard_map/reduce_scatter | solution.py:204
  646.8 23.2 %copy-start.1 = (f32[1,2,256,16,64]{2,0,1,4,3:T(1,128)}, f32[1,2,256,16,64]{2,0,1,4,3:T(1,128)S(1)}, u32[]{:S(2)}) copy-start(f32[1,2,256,16,64]{2,0,1,4,3:T(1,128)S(1)} %constant_dynamic-slice_fusion.13) | copy-start | bytes 6291460 | tf_op jit(solution)/shard_map/transpose(jvp())/while
  772.4 23.2 %copy-start.1 = (f32[1,2,256,16,64]{2,0,1,4,3:T(1,128)}, f32[1,2,256,16,64]{2,0,1,4,3:T(1,128)S(1)}, u32[]{:S(2)}) copy-start(f32[1,2,256,16,64]{2,0,1,4,3:T(1,128)S(1)} %constant_dynamic-slice_fusion.13) | copy-start | bytes 6291460 | tf_op jit(solution)/shard_map/transpose(jvp())/while
  869.2 16.8 copy-start.2
  869.2 16.8 copy-start.3
  909.6 23.2 %copy-start.1 = (f32[1,2,256,16,64]{2,0,1,4,3:T(1,128)}, f32[1,2,256,16,64]{2,0,1,4,3:T(1,128)S(1)}, u32[]{:S(2)}) copy-start(f32[1,2,256,16,64]{2,0,1,4,3:T(1,128)S(1)} %constant_dynamic-slice_fusion.13) | copy-start | bytes 6291460 | tf_op jit(solution)/shard_map/transpose(jvp())/while
  1035.2 23.2 %copy-start.1 = (f32[1,2,256,16,64]{2,0,1,4,3:T(1,128)}, f32[1,2,256,16,64]{2,0,1,4,3:T(1,128)S(1)}, u32[]{:S(2)}) copy-start(f32[1,2,256,16,64]{2,0,1,4,3:T(1,128)S(1)} %constant_dynamic-slice_fusion.13) | copy-start | bytes 6291460 | tf_op jit(solution)/shard_map/transpose(jvp())/while
  1175.0 20.0 %copy-start.56 = (f32[16]{0:T(128)}, f32[16]{0:T(128)S(1)}, u32[]{:S(2)}) copy-start(f32[16]{0:T(128)S(1)} %get-tuple-element.1213) | copy-start | bytes 196
  1175.0 18.5 %copy-start.19 = (f32[4,2,256,128]{3,2,1,0:T(8,128)S(1)}, f32[4,2,256,128]{3,2,1,0:T(8,128)}, u32[]{:S(2)}) copy-start(f32[4,2,256,128]{3,2,1,0:T(8,128)} %get-tuple-element.1210) | copy-start | bytes 3145732
  1176.4 18.7 %copy-start.52 = (f32[2048]{0:T(1024)S(1)}, f32[2048]{0:T(1024)}, u32[]{:S(2)}) copy-start(f32[2048]{0:T(1024)} %copy-done.51) | copy-start | bytes 24580
  1176.4 18.7 %copy-start.65 = (f32[1024]{0:T(1024)S(1)}, f32[1024]{0:T(1024)}, u32[]{:S(2)}) copy-start(f32[1024]{0:T(1024)} %param.40) | copy-start | bytes 12292
  1195.0 236.7 %reduce-scatter.3.cloned.1.call-start = ((), (), s32[]{:S(2)}) async-start(), calls=%async_computation.4 | async-start | bytes 12582912 | tf_op jit(solution)/shard_map/reduce_scatter | solution.py:173
  1207.0 230.6 %all-reduce.16.cloned.1.call-start = ((), (), s32[]{:S(2)}) async-start(), calls=%async_computation.7 | async-start | bytes 16777216 | tf_op jit(solution)/shard_map/psum | solution.py:237
  1257.7 46.3 %copy-start.25 = (f32[2,1024,16]{1,2,0:T(8,128)S(1)}, f32[2,1024,16]{1,2,0:T(8,128)}, u32[]{:S(2)}) copy-start(f32[2,1024,16]{1,2,0:T(8,128)} %copy-done.24) | copy-start | bytes 393220
  1257.7 46.3 %copy-start.42 = (u8[1024,16]{0,1:T(8,128)(4,1)S(1)}, u8[1024,16]{0,1:T(8,128)(4,1)}, u32[]{:S(2)}) copy-start(u8[1024,16]{0,1:T(8,128)(4,1)} %copy-done.41) | copy-start | bytes 49156
  1257.7 46.3 %copy-start.54 = (f32[16]{0:T(128)S(1)}, f32[16]{0:T(128)}, u32[]{:S(2)}) copy-start(f32[16]{0:T(128)} %copy-done.53) | copy-start | bytes 196
  1257.7 46.3 %copy-start.58 = (u8[1024,16]{0,1:T(8,128)(4,1)S(1)}, u8[1024,16]{0,1:T(8,128)(4,1)}, u32[]{:S(2)}) copy-start(u8[1024,16]{0,1:T(8,128)(4,1)} %get-tuple-element.1925) | copy-start | bytes 49156
  1257.7 46.5 %copy-start.50 = (bf16[1024,16]{0,1:T(8,128)(2,1)S(1)}, bf16[1024,16]{0,1:T(8,128)(2,1)}, u32[]{:S(2)}) copy-start(bf16[1024,16]{0,1:T(8,128)(2,1)} %param.32) | copy-start | bytes 98308
  1320.9 26.1 %copy-start.34 = (f32[1152]{0:T(1024)S(1)}, f32[1152]{0:T(1024)}, u32[]{:S(2)}) copy-start(f32[1152]{0:T(1024)} %copy-done.33) | copy-start | bytes 13828
  1320.9 26.1 %copy-start.36 = (f32[1152]{0:T(1024)S(1)}, f32[1152]{0:T(1024)}, u32[]{:S(2)}) copy-start(f32[1152]{0:T(1024)} %copy-done.35) | copy-start | bytes 13828
  1320.9 26.1 %copy-start.38 = (f32[1152]{0:T(1024)S(1)}, f32[1152]{0:T(1024)}, u32[]{:S(2)}) copy-start(f32[1152]{0:T(1024)} %copy-done.37) | copy-start | bytes 13828
  1320.9 26.1 %copy-start.40 = (f32[1152]{0:T(1024)S(1)}, f32[1152]{0:T(1024)}, u32[]{:S(2)}) copy-start(f32[1152]{0:T(1024)} %copy-done.39) | copy-start | bytes 13828
  1358.4 13.5 collective-permute-start.1
  1371.9 17.7 slice-start
  1371.9 17.7 slice-start.2
  1398.2 427.4 %all-reduce.18.cloned.1.call-start = ((), (), s32[]{:S(2)}) async-start(), calls=%async_computation.10 | async-start | bytes 26345472 | tf_op jit(solution)/shard_map/psum | solution.py:245
  1398.4 24.1 %slice-start.4 = ((s8[4718592]{0:T(1024)(128)(4,1)}), s8[4194304]{0:T(1024)(128)(4,1)S(1)}, s32[]{:S(2)}) async-start(s8[4718592]{0:T(1024)(128)(4,1)} %bitcast.688), calls=%async_computation.15 | async-start | bytes 8388608
  (64 other events, 623.5 us)
Sparse Core Ops, SparseCore 0:
  9.6 16.3 all-gather.9
  90.3 12.0 all-gather.11
  240.0 82.4 all-gather.15
  323.9 12.1 all-gather.13
  471.2 79.1 all-gather.17
  1195.1 8.0 reduce-scatter.4
  1207.1 16.4 reduce-scatter.2
  1398.3 39.2 all-reduce.15
  1445.2 380.3 all-reduce.17
where the time goes:
time: 1860 us; the launch traced here: 1840 us
  matrix products  581 us (31%)
  local copies, waits for them, and re-layouts  389 us (21%)
  other arithmetic  388 us (21%)
  waiting for transfers between devices  353 us (19%)
  blocking collectives  101 us (5%)
    psum x1, waiting for transfers between devices, per_device(): lax.psum((grad_norm_gain, grad_proj_gate, grad_proj_values, grad_proj_sta...  291 us
    dot_general x12, matrix products, span_step(): jnp.einsum('stuh,suhp->sthp', mixing, block_values, precision=highest)  251 us
    dynamic_slice x24, local copies, waits for them, and re-layouts, span_scan(): lax.scan(span_step, start, (by_block(values), by_block(steps), by_block(w...  118 us
    psum x1, blocking collectives, per_device(): lax.psum((grad_norm_gain, grad_proj_gate, grad_proj_values, grad_proj_sta...  82.1 us
    another operation x45, other arithmetic  79 us
    dynamic_update_slice x20, other arithmetic, span_scan(): lax.scan(span_step, start, (by_block(values), by_block(steps), by_block(w...  75.5 us
    dot_general x16, matrix products, span_step(): jnp.einsum('suh,suhp,sun->shpn', tail, block_values, block_writes, precis...  69.6 us
    dot_general x16, matrix products, span_step(): jnp.einsum('stn,shpn->sthp', block_reads, state, precision=highest)  68.8 us
  transfers between devices with their start and end apart: 11, of which 5 were waited for; matrix products, arithmetic and copies ran while one was open for 30% of the time, Pallas kernels for 0%

commit v1 on v0

v1 whole, which is shorter than its diff:
```python
import functools

import jax
import jax.numpy as jnp
from jax import lax
from jax.experimental import pallas as pl
from jax.experimental.pallas import tpu as pltpu
from jax.sharding import PartitionSpec as P

CHUNK = 128
LANES = 128
epsilon = 1e-05
highest = lax.Precision.HIGHEST
f32 = jnp.float32
bf16 = jnp.bfloat16


def mm(a, b, dims=((1,), (0,))):
    return lax.dot_general(a, b, (dims, ((), ())), preferred_element_type=f32)


def split_mm(a, b):
    high = a.astype(bf16)
    low = (a - high.astype(f32)).astype(bf16)
    return mm(high, b) + mm(low, b)


def pair_decays(cum_ref, cumt_ref, j, causal):
    parts = []
    for h in (2 * j, 2 * j + 1):
        differ = cum_ref[0, :, h : h + 1] - cumt_ref[0, h : h + 1, :]
        parts.append(jnp.exp(jnp.where(causal, differ, -1e30)))
    return parts


def spread(column_ref, j, first):
    return jnp.where(
        first, column_ref[0, :, 2 * j : 2 * j + 1], column_ref[0, :, 2 * j + 1 : 2 * j + 2]
    )


def causal_mask():
    rows = lax.broadcasted_iota(jnp.int32, (CHUNK, CHUNK), 0)
    columns = lax.broadcasted_iota(jnp.int32, (CHUNK, CHUNK), 1)
    return rows >= columns


def forward_kernel(x_ref, st_ref, cum_ref, cumt_ref, b_ref, c_ref, skip_ref, enter_ref,
                   core_ref, states_ref, state):
    pairs = x_ref.shape[2] // LANES

    @pl.when(pl.program_id(1) == 0)
    def _():
        state[...] = enter_ref[0]

    causal = causal_mask()
    first = lax.broadcasted_iota(jnp.int32, (CHUNK, LANES), 1) < LANES // 2
    first_row = lax.broadcasted_iota(jnp.int32, (LANES, LANES), 0) < LANES // 2
    writes, reads = b_ref[0], c_ref[0]
    scores = mm(reads, writes, ((1,), (1,)))
    for j in range(pairs):
        at = slice(j * LANES, (j + 1) * LANES)
        x = x_ref[0, :, at]
        scaled = (x * spread(st_ref, j, first)).astype(bf16)
        zero = jnp.zeros_like(scaled)
        left, right = pair_decays(cum_ref, cumt_ref, j, causal)
        mixing = jnp.concatenate(
            [(left * scores).astype(bf16), (right * scores).astype(bf16)], axis=1
        )
        stacked = jnp.concatenate(
            [jnp.where(first, scaled, zero), jnp.where(first, zero, scaled)], axis=0
        )
        cum = spread(cum_ref, j, first)
        last = cum[CHUNK - 1 :, :]
        entered = state[at, :].astype(bf16)
        states_ref[0, 0, at, :] = entered
        carried = mm(reads, entered, ((1,), (1,))) * jnp.exp(cum)
        core_ref[0, :, at] = mm(mixing, stacked) + carried + skip_ref[:, at] * x
        weighted = (scaled.astype(f32) * jnp.exp(last - cum)).astype(bf16)
        fresh = mm(weighted, writes, ((0,), (0,)))
        end = CHUNK - 1
        decay = jnp.exp(
            jnp.where(
                first_row,
                cum_ref[0, end:, 2 * j : 2 * j + 1],
                cum_ref[0, end:, 2 * j + 1 : 2 * j + 2],
            )
        )
        state[at, :] = state[at, :] * decay + fresh


def backward_kernel(x_ref, dy_ref, core_ref, st_ref, cum_ref, cumt_ref, b_ref, c_ref, skip_ref,
                    states_ref, later_ref, pick_ref,
                    dx_ref, maps_ref, direct_ref, decay_ref,
                    state, state_low, grown, shrunk, balance, product):
    pairs = x_ref.shape[2] // LANES

    @pl.when(pl.program_id(1) == 0)
    def _():
        state[...] = later_ref[0]

    causal = causal_mask()
    first = lax.broadcasted_iota(jnp.int32, (CHUNK, LANES), 1) < LANES // 2
    first_row = lax.broadcasted_iota(jnp.int32, (LANES, LANES), 0) < LANES // 2
    end = CHUNK - 1
    at_end = lax.broadcasted_iota(jnp.int32, (CHUNK, LANES), 0) == end
    writes, reads = b_ref[0], c_ref[0]
    scores = mm(reads, writes, ((1,), (1,)))
    ones = jnp.ones((8, LANES), bf16)
    score_grad = jnp.zeros((CHUNK, CHUNK), f32)
    for j in range(pairs):
        at = slice(j * LANES, (j + 1) * LANES)
        x = x_ref[0, :, at]
        dy = dy_ref[0, :, at]
        step = spread(st_ref, j, first)
        scaled = (x * step).astype(bf16)
        low = dy.astype(bf16)
        zero = jnp.zeros_like(low)
        left, right = pair_decays(cum_ref, cumt_ref, j, causal)
        split = jnp.concatenate(
            [jnp.where(first, low, zero), jnp.where(first, zero, low)], axis=0
        )
        mixing = jnp.concatenate(
            [(left * scores).astype(bf16), (right * scores).astype(bf16)], axis=0
        )
        mixing_grad = mm(split, scaled, ((1,), (1,)))
        score_grad = score_grad + mixing_grad[:CHUNK] * left + mixing_grad[CHUNK:] * right
        cum = spread(cum_ref, j, first)
        last = cum[end:, :]
        grow = jnp.exp(cum)
        shrink = jnp.exp(last - cum)
        later = state[at, :]
        later_low = later.astype(bf16)
        state_low[at, :] = later_low
        through = mm(writes, later_low, ((1,), (1,))) * shrink
        scaled_grad = mm(mixing, split, ((0,), (0,))) + through
        skip = skip_ref[:, at]
        dx_ref[0, :, at] = step * scaled_grad + skip * dy
        kept = scaled.astype(f32)
        entered = states_ref[0, 0, at, :]
        meet = mm(ones, (later * entered.astype(f32)).astype(bf16), ((1,), (1,)))[0:1, :]
        finish = jnp.sum(kept * through, axis=0, keepdims=True) + jnp.exp(last) * meet
        terms = low.astype(f32) * (core_ref[0, :, at] - skip * x) - kept * scaled_grad
        balance[:, at] = terms + jnp.where(at_end, finish, 0.0)
        product[:, at] = x * scaled_grad
        grown_here = (dy * grow).astype(bf16)
        grown[:, at] = grown_here
        shrunk[:, at] = (kept * shrink).astype(bf16)
        decay = jnp.exp(
            jnp.where(
                first_row,
                cum_ref[0, end:, 2 * j : 2 * j + 1],
                cum_ref[0, end:, 2 * j + 1 : 2 * j + 2],
            )
        )
        state[at, :] = later * decay + mm(grown_here, reads, ((0,), (0,)))
    score_low = score_grad.astype(bf16)
    maps_ref[0, :, LANES:] = mm(score_low, writes) + mm(grown[...], states_ref[0, 0])
    maps_ref[0, :, :LANES] = mm(score_low, reads, ((0,), (0,))) + mm(shrunk[...], state_low[...])
    direct_ref[0] = split_mm(product[...], pick_ref[...])
    sums = split_mm(balance[...], pick_ref[...])
    upper = lax.broadcasted_iota(jnp.int32, (CHUNK, CHUNK), 0) <= lax.broadcasted_iota(
        jnp.int32, (CHUNK, CHUNK), 1
    )
    upper = upper.astype(f32)
    decay_ref[0] = jnp.dot(upper, sums, precision=highest, preferred_element_type=f32)


def whole_block(array):
    return pl.BlockSpec(array.shape, lambda g, c: (0,) * array.ndim)


def run_forward(values, steps, cum, cumt, writes, reads, skip, entering):
    groups, length, inner = values.shape
    heads, size = steps.shape[2], writes.shape[2]
    chunks = length // CHUNK

    def rows(width):
        return pl.BlockSpec((1, CHUNK, width), lambda g, c: (g, c, 0))

    return pl.pallas_call(
        forward_kernel,
        grid=(groups, chunks),
        in_specs=[
            rows(inner), rows(heads), rows(heads),
            pl.BlockSpec((1, heads, CHUNK), lambda g, c: (g, 0, c)),
            rows(size), rows(size), whole_block(skip),
            pl.BlockSpec((1, inner, size), lambda g, c: (g, 0, 0)),
        ],
        out_specs=[
            rows(inner),
            pl.BlockSpec((1, 1, inner, size), lambda g, c: (g, c, 0, 0)),
        ],
        out_shape=[
            jax.ShapeDtypeStruct(values.shape, f32),
            jax.ShapeDtypeStruct((groups, chunks, inner, size), bf16),
        ],
        scratch_shapes=[pltpu.VMEM((inner, size), f32)],
        compiler_params=pltpu.CompilerParams(vmem_limit_bytes=40 * 1024 * 1024),
        cost_estimate=pl.CostEstimate(
            flops=20_000_000_000, bytes_accessed=30_000_000, transcendentals=0
        ),
        name="recurrence_forward",
    )(values, steps, cum, cumt, writes, reads, skip, entering)


def run_backward(values, back, core, steps, cum, cumt, writes, reads, skip, states, later, pick):
    groups, length, inner = values.shape
    heads, size = steps.shape[2], writes.shape[2]
    chunks = length // CHUNK

    def rows(width):
        return pl.BlockSpec((1, CHUNK, width), lambda g, c: (g, chunks - 1 - c, 0))

    return pl.pallas_call(
        backward_kernel,
        grid=(groups, chunks),
        in_specs=[
            rows(inner), rows(inner), rows(inner), rows(heads), rows(heads),
            pl.BlockSpec((1, heads, CHUNK), lambda g, c: (g, 0, chunks - 1 - c)),
            rows(size), rows(size), whole_block(skip),
            pl.BlockSpec((1, 1, inner, size), lambda g, c: (g, chunks - 1 - c, 0, 0)),
            pl.BlockSpec((1, inner, size), lambda g, c: (g, 0, 0)),
            whole_block(pick),
        ],
        out_specs=[rows(inner), rows(2 * size), rows(heads), rows(heads)],
        out_shape=[
            jax.ShapeDtypeStruct(values.shape, f32),
            jax.ShapeDtypeStruct((groups, length, 2 * size), f32),
            jax.ShapeDtypeStruct(steps.shape, f32),
            jax.ShapeDtypeStruct(steps.shape, f32),
        ],
        scratch_shapes=[
            pltpu.VMEM((inner, size), f32),
            pltpu.VMEM((inner, size), bf16),
            pltpu.VMEM((CHUNK, inner), bf16),
            pltpu.VMEM((CHUNK, inner), bf16),
            pltpu.VMEM((CHUNK, inner), f32),
            pltpu.VMEM((CHUNK, inner), f32),
        ],
        compiler_params=pltpu.CompilerParams(vmem_limit_bytes=40 * 1024 * 1024),
        cost_estimate=pl.CostEstimate(
            flops=60_000_000_000, bytes_accessed=45_000_000, transcendentals=0
        ),
        name="recurrence_backward",
    )(values, back, core, steps, cum, cumt, writes, reads, skip, states, later, pick)


def from_behind(block, axis, distance):
    devices = range(lax.axis_size(axis))
    route = [(i - distance, i) for i in devices if i - distance in devices]
    return lax.ppermute(block, axis, route)


def reached_state(total, part, axis, reverse, head_width):
    length, index = lax.axis_size(axis), lax.axis_index(axis)
    totals = lax.all_gather(total, axis)
    parts = lax.all_gather(part.astype(bf16), axis)
    result = jnp.zeros(part.shape, f32)
    for k in range(length):
        at = length - 1 - k if reverse else k
        used = at > index if reverse else at < index
        decay = jnp.repeat(jnp.exp(totals[at]), head_width, axis=1)[:, :, None]
        result = jnp.where(used, result * decay + parts[at].astype(f32), result)
    return result


def half_sum(terms):
    if lax.axis_size("head") != 2:
        return lax.psum_scatter(terms, "head", scatter_dimension=1, tiled=True)
    here, half = lax.axis_index("head"), terms.shape[1] // 2
    mine = lax.dynamic_slice_in_dim(terms, here * half, half, 1)
    theirs = lax.dynamic_slice_in_dim(terms, (1 - here) * half, half, 1)
    got = lax.ppermute(theirs.astype(bf16), "head", [(0, 1), (1, 0)])
    return mine + got.astype(f32)


def silu_slope(value):
    logistic = jax.nn.sigmoid(value)
    return logistic * (1.0 + value * (1.0 - logistic))


def convolve(signal, edges, kernel, offset):
    padded = jnp.concatenate([edges, signal], axis=1)
    length = signal.shape[1]
    result = offset + kernel[0] * padded[:, 0:length]
    for position in range(1, kernel.shape[0]):
        result = result + kernel[position] * padded[:, position : position + length]
    return result


def summed_after(part, earlier):
    low = part.astype(bf16)
    if earlier is not None:
        low, earlier = lax.optimization_barrier((low, earlier))
    return lax.psum(low, ("batch", "seq")), earlier


def per_device(
    hidden,
    cotangent,
    norm_gain,
    proj_gate,
    proj_values,
    proj_state,
    proj_steps,
    conv_values,
    conv_state,
    bias_values,
    bias_state,
    step_bias,
    log_rates,
    skip_gain,
    gate_gain,
    proj_output,
):
    groups, length, width_share = hidden.shape
    tokens = groups * length
    whole_rows, gain_whole = (
        lax.all_gather(hidden, "head", axis=2, tiled=True),
        lax.all_gather(norm_gain, "head", axis=0, tiled=True),
    )
    cot_whole = lax.all_gather(cotangent, "head", axis=2, tiled=True).reshape(tokens, -1)
    inputs = whole_rows.astype(f32).reshape(tokens, -1)
    width_full = inputs.shape[1]
    gain_float = gain_whole.astype(f32)
    inv_rms = lax.rsqrt(jnp.mean(inputs * inputs, axis=1, keepdims=True) + epsilon)
    normed = (inputs * inv_rms * gain_float).astype(bf16)
    value_pre = mm(normed, proj_values)
    state_pre = mm(normed, proj_state)
    steps_pre = mm(normed, proj_steps)
    gate_pre = mm(normed, proj_gate)
    inner_share = value_pre.shape[1]
    heads_here = steps_pre.shape[1]
    headdim = inner_share // heads_here
    margin = conv_values.shape[0] - 1

    def conv_in(pre, kernel, offset):
        shaped = pre.reshape(groups, length, -1)
        edges = from_behind(shaped[:, length - margin :], "seq", 1)
        return shaped, edges, convolve(shaped, edges, kernel, offset)

    state_mixed, state_edges, state_conv = conv_in(state_pre, conv_state, bias_state)
    value_mixed, value_edges, value_conv = conv_in(value_pre, conv_values, bias_values)
    values = jax.nn.silu(value_conv)
    maps_full = lax.all_gather(jax.nn.silu(state_conv).astype(bf16), "head", axis=2, tiled=True)
    state_size = maps_full.shape[2] // 2
    writes = maps_full[:, :, :state_size]
    reads = maps_full[:, :, state_size:]
    dt_raw = steps_pre.reshape(groups, length, heads_here)
    steps = jax.nn.softplus(dt_raw + step_bias)
    rates = -jnp.exp(log_rates)
    chunks = length // CHUNK
    lower = jnp.tril(jnp.ones((CHUNK, CHUNK), f32))
    cum4 = jnp.einsum(
        "tu,gcuh->gcth",
        lower,
        (steps * rates).reshape(groups, chunks, CHUNK, heads_here),
        precision=highest,
    )
    cum = cum4.reshape(groups, length, heads_here)
    cumt = jnp.swapaxes(cum, 1, 2)
    ends = cum4[:, :, -1]
    prefix = [jnp.zeros_like(ends[:, 0])]
    for c in range(chunks):
        prefix.append(prefix[-1] + ends[:, c])
    total_log = prefix[-1]
    cumseg = (cum4 + jnp.stack(prefix[:-1], axis=1)[:, :, None]).reshape(cum.shape)

    def lanes(array):
        return jnp.repeat(array, headdim, axis=-1)

    tail = jnp.exp(total_log[:, None] - cumseg) * steps
    zero_final = jnp.einsum(
        "glp,gln->gpn", (values * lanes(tail)).astype(bf16), writes, preferred_element_type=f32
    )
    entering = reached_state(total_log, zero_final, "seq", False, headdim)
    skip = lanes(skip_gain)[None]
    core3, states = run_forward(values, steps, cum, cumt, writes, reads, skip, entering)
    core = core3.reshape(tokens, inner_share)
    gate_act = jax.nn.silu(gate_pre)
    gated = core * gate_act
    square_sum = lax.psum(jnp.sum(gated * gated, axis=1), "head")
    inner_full = inner_share * lax.axis_size("head")
    inv_gate = lax.rsqrt(square_sum / inner_full + epsilon)[:, None]
    gate_unit = gated * inv_gate
    gate_normed = (gate_unit * gate_gain).astype(bf16)
    grad_proj_output = mm(gate_normed, cot_whole, ((0,), (0,)))
    sum_proj_output, _ = summed_after(grad_proj_output, None)
    out_share = half_sum(mm(gate_normed, proj_output))
    block_out = (hidden.astype(f32) + out_share.reshape(hidden.shape)).astype(bf16)
    back_gnorm = mm(cot_whole, proj_output, ((1,), (1,)))
    grad_gate_gain = jnp.sum(back_gnorm * gate_unit, axis=0)
    scaled_gate = back_gnorm * gate_gain
    gate_inner = lax.psum(jnp.sum(scaled_gate * gate_unit, axis=1), "head")
    back_gated = inv_gate * (scaled_gate - gate_unit * (gate_inner / inner_full)[:, None])
    back_core = (back_gated * gate_act).reshape(groups, length, inner_share)
    back_gate = (back_gated * core * silu_slope(gate_pre)).astype(bf16)
    grad_skip_gain = jnp.sum(
        jnp.sum(back_core * values, axis=(0, 1)).reshape(heads_here, headdim), axis=1
    )
    entry_grad = jnp.einsum(
        "glp,gln->gpn",
        (back_core * lanes(jnp.exp(cumseg))).astype(bf16),
        reads,
        preferred_element_type=f32,
    )
    later_grad = reached_state(total_log, entry_grad, "seq", True, headdim)
    grad_proj_gate = mm(normed, back_gate, ((0,), (0,)))
    sum_proj_gate, sum_proj_output = summed_after(grad_proj_gate, sum_proj_output)
    pick = (
        jnp.arange(inner_share)[:, None] // headdim == jnp.arange(heads_here)[None, :]
    ).astype(bf16)
    back_values, back_maps_local, direct, decay_grad = run_backward(
        values, back_core, core3, steps, cum, cumt, writes, reads, skip, states, later_grad, pick
    )
    back_steps = direct + rates * decay_grad
    grad_log_rates = rates * jnp.sum(steps * decay_grad, axis=(0, 1))
    back_dt = back_steps * jax.nn.sigmoid(dt_raw + step_bias)
    grad_step_bias = jnp.sum(back_dt, axis=(0, 1))
    back_maps = half_sum(back_maps_local.reshape(tokens, -1)).reshape(groups, length, -1)

    def conv_out(back_act, conv_pre, mixed, edges, kernel, offset):
        back_conv = back_act * silu_slope(conv_pre)
        padded = jnp.concatenate([edges, mixed], axis=1)
        taps = jnp.stack(
            [
                jnp.sum(back_conv * padded[:, k : k + length], axis=(0, 1))
                for k in range(margin + 1)
            ]
        )
        ahead = from_behind(back_conv[:, :margin], "seq", -1)
        extended = jnp.concatenate([back_conv, ahead], axis=1)
        back = kernel[margin] * back_conv
        for k in range(margin):
            back = back + kernel[k] * extended[:, margin - k : margin - k + length]
        return back.reshape(tokens, -1).astype(bf16), taps, jnp.sum(back_conv, axis=(0, 1))

    back_value_pre, grad_conv_values, grad_bias_values = conv_out(
        back_values, value_conv, value_mixed, value_edges, conv_values, bias_values
    )
    back_state_pre, grad_conv_state, grad_bias_state = conv_out(
        back_maps, state_conv, state_mixed, state_edges, conv_state, bias_state
    )
    back_steps_pre = back_dt.reshape(tokens, heads_here).astype(bf16)
    grad_proj_values = mm(normed, back_value_pre, ((0,), (0,)))
    sum_proj_values, sum_proj_gate = summed_after(grad_proj_values, sum_proj_gate)
    grad_proj_state = mm(normed, back_state_pre, ((0,), (0,)))
    grad_proj_steps = mm(normed, back_steps_pre, ((0,), (0,)))
    across = ((1,), (1,))
    back_normed = mm(back_gate, proj_gate, across) + mm(back_value_pre, proj_values, across)
    back_normed = back_normed + mm(back_state_pre, proj_state, across)
    back_normed = back_normed + mm(back_steps_pre, proj_steps, across)
    normed_total = half_sum(back_normed)
    unit_here = hidden.astype(f32).reshape(tokens, width_share) * inv_rms
    scaled_input = normed_total * norm_gain.astype(f32)
    input_inner = lax.psum(jnp.sum(scaled_input * unit_here, axis=1), "head") / width_full
    back_input = inv_rms * (scaled_input - unit_here * input_inner[:, None])
    grad_norm_gain = jnp.sum(normed_total * unit_here, axis=0)
    grad_hidden = cotangent.astype(f32) + back_input.reshape(hidden.shape)
    small = lax.psum(
        (
            grad_proj_state,
            grad_proj_steps,
            grad_conv_values,
            grad_conv_state,
            grad_bias_values,
            grad_bias_state,
            grad_step_bias,
            grad_log_rates,
            grad_skip_gain,
            grad_gate_gain,
            grad_norm_gain,
        ),
        ("batch", "seq"),
    )
    return (
        block_out,
        grad_hidden,
        small[10],
        sum_proj_gate.astype(f32),
        sum_proj_values.astype(f32),
    ) + small[:10] + (sum_proj_output.astype(f32),)


def solution(mesh):
    in_specs = (
        P("batch", "seq", "head"),
        P("batch", "seq", "head"),
        P("head"),
        P(None, "head"),
        P(None, "head"),
        P(None, "head"),
        P(None, "head"),
        P(None, "head"),
        P(None, "head"),
        P("head"),
        P("head"),
        P("head"),
        P("head"),
        P("head"),
        P("head"),
        P("head", None),
    )
    out_specs = (
        P("batch", "seq", "head"),
        P("batch", "seq", "head"),
        P("head"),
        P(None, "head"),
        P(None, "head"),
        P(None, "head"),
        P(None, "head"),
        P(None, "head"),
        P(None, "head"),
        P("head"),
        P("head"),
        P("head"),
        P("head"),
        P("head"),
        P("head"),
        P("head", None),
    )
    return jax.shard_map(
        per_device, mesh=mesh, in_specs=in_specs, out_specs=out_specs, check_vma=False
    )
```

time: 1860 us -> 787 us (0.42)
  matrix products: 581 us -> 130 us
  local copies, waits for them, and re-layouts: 389 us -> 76.1 us
  other arithmetic: 388 us -> 144 us
  waiting for transfers between devices: 353 us -> 234 us
  Pallas kernels: 0 us -> 68.5 us
    dot_general x78 -> x18, matrix products: 581 us -> 130 us  [the longest x15 110 us: mm(): return lax.dot_general(a, b, (dims, ((), ())), preferred_element_type=f32)]
    dynamic_slice x25 -> x0, local copies, waits for them, and re-layouts: 118 us -> none  [the longest x24 118 us: span_scan(): lax.scan(span_step, start, (by_block(values), by_block(steps), by_block(w...]
    psum x2 -> x4, waiting for transfers between devices: 291 us -> 177 us  [the longest x1 112 us: per_device(): lax.psum((grad_proj_state, grad_proj_steps, grad_conv_values, grad_conv_s...]
    another operation x45 -> x4, other arithmetic: 79 us -> 2.63 us  [the longest x2 2.6 us: reached_state(): result = jnp.where(used, result * decay + parts[at].astype(f32), result)]
    dynamic_update_slice x20 -> x0, other arithmetic: 75.5 us -> none  [span_scan(): lax.scan(span_step, start, (by_block(values), by_block(steps), by_block(w...]
    reshape x10 -> x4, local copies, waits for them, and re-layouts: 90.1 us -> 21 us  [the longest x2 17.4 us: lanes(): return jnp.repeat(array, headdim, axis=-1)]
    pallas_call x0 -> x2, Pallas kernels: none -> 68.5 us  [the longest x1 44.3 us: run_backward(): pl.pallas_call(backward_kernel, grid=(groups, chunks), in_specs=[rows(inn...]
    another operation x59 -> x3, local copies, waits for them, and re-layouts: 54.2 us -> 0.11 us  [the longest x1 0.08 us: per_device(): skip = lanes(skip_gain)[None]]
  transfers between devices with their start and end apart: 11 -> 16, of which waited for: 5 -> 6; matrix products, arithmetic and copies ran while one was open for 30% -> 40% of each run, Pallas kernels for 0% -> 9%
where the time goes in v1:
time: 787 us; the launch traced here: 776 us
  waiting for transfers between devices  234 us (30%)
  other arithmetic  144 us (18%)
  matrix products  130 us (17%)
  blocking collectives  96.5 us (12%)
  local copies, waits for them, and re-layouts  76.1 us (10%)
  Pallas kernels  68.5 us (9%)
  between operations  15.1 us (2%)
  starting transfers between devices  11.8 us (1%)
    psum x1, waiting for transfers between devices, per_device(): lax.psum((grad_proj_state, grad_proj_steps, grad_conv_values, grad_conv_s...  112 us
    dot_general x15, matrix products, mm(): return lax.dot_general(a, b, (dims, ((), ())), preferred_element_type=f32)  110 us
    psum x1, blocking collectives, per_device(): lax.psum((grad_proj_state, grad_proj_steps, grad_conv_values, grad_conv_s...  76.8 us
    psum x3, waiting for transfers between devices, summed_after(): return (lax.psum(low, ('batch', 'seq')), earlier)  65.6 us
    pallas_call x1, Pallas kernels, run_backward(): pl.pallas_call(backward_kernel, grid=(groups, chunks), in_specs=[rows(inn...  44.3 us
    all_gather x2, waiting for transfers between devices, reached_state(): parts = lax.all_gather(part.astype(bf16), axis)  42.7 us
    pallas_call x1, Pallas kernels, run_forward(): pl.pallas_call(forward_kernel, grid=(groups, chunks), in_specs=[rows(inne...  24.3 us
    reduce_sum x2, other arithmetic, conv_out(): jnp.sum(back_conv * padded[:, k:k + length], axis=(0, 1))  21.4 us
  transfers between devices with their start and end apart: 16, of which 6 were waited for; matrix products, arithmetic and copies ran while one was open for 40% of the time, Pallas kernels for 9%

profile of v1, /device:TPU:0, one launch (start us, length us, event | category | flops | bytes accessed | tf_op | source)
XLA Modules:
  0.0 776.1 jit_solution(11010161786236567429)
XLA Ops:
  13.1 12.9 %all-gather.10.cloned.1.call-done = bf16[2,1024,1024]{2,1,0:T(8,128)(2,1)} async-done(((bf16[2,1024,512]{2,1,0:T(8,128)(2,1)}), bf16[2,1024,1024]{2,1,0:T(8,128)(2,1)}) %all-gather.10.cloned.1.call-update) | async-done | bytes 4194320 | tf_op jit(solution)/shard_map/all_gather | solution.py:320
  26.0 3.2 multiply_reduce_fusion.8
  29.9 3.5 fusion.49
  34.4 3.6 collective-permute-start.1
  43.7 10.8 %fusion.20 = f32[2,1024,1024]{2,1,0:T(8,128)} fusion(bf16[1024,1024]{1,0:T(8,128)(2,1)} %param.20, f32[1024]{0:T(1024)S(1)} %bitcast.153, f32[2,1024]{1,0:T(2,128)S(1)} %get-tuple-element.94, bf16[2,1024,1024]{2,1,0:T(8,128)(2,1)} %all-gather.10.cloned.1.call-done), kind=kOutput, calls=%fused_computation.59 | convolution fusion | flops 4303355904 | bytes 14692352 | tf_op jit(solution)/shard_map/dot_general | solution.py:19
  57.6 4.4 broadcast_in_dim.24
  62.0 8.7 %copy.78 = f32[2,1024,1024]{2,1,0:T(8,128)} copy(f32[2,1024,1024]{1,2,0:T(8,128)} %bitcast.129) | data formatting | bytes 16777216 | tf_op jit(solution)/shard_map/reshape | solution.py:371
  71.5 3.7 collective-permute-start
  75.3 4.3 multiply_convert_fusion.10
  79.7 18.0 %fusion.16 = (f32[2,1024,1024]{2,1,0:T(8,128)}, f32[2,1024,1024]{2,1,0:T(8,128)}) fusion(f32[2,1024,1024]{2,1,0:T(8,128)} %fusion.20, f32[1024]{0:T(1024)S(1)} %bitcast.147, f32[2,3,1024]{2,1,0:T(4,128)S(1)} %collective-permute-done, f32[1024]{0:T(1024)S(1)} %bitcast.149, f32[1024]{0:T(1024)S(1)} %bitcast.145, f32[1024]{0:T(1024)S(1)} %bitcast.143, ...), kind=kLoop, calls=%fused_computation.41 | loop fusion | flops 31457280 | bytes 25210880 | tf_op jit(solution)/shard_map/jit(silu)/mul | solution.py:345
  97.8 9.6 %fusion.23 = bf16[2,1024,128]{2,1,0:T(8,128)(2,1)} fusion(f32[2,1024,1024]{2,1,0:T(8,128)} %copy.78, bf16[2,1024,256]{2,1,0:T(8,128)(2,1)} %all-gather.12.cloned.1.call-done, f32[2,1024,1024]{2,1,0:T(8,128)} %get-tuple-element.81), kind=kOutput, calls=%fused_computation.69 | convolution fusion | flops 549715968 | bytes 17825792 | tf_op jit(solution)/shard_map/glp,gln->gpn/dot_general | solution.py:374
  109.0 9.1 %all-gather = f32[8,1,16]{2,1,0:T(1,128)S(1)} all-gather(f32[2,1,16]{2,1,0:T(1,128)S(1)} %get-tuple-element.69), channel_id=2, replica_groups=mesh['batch'=4,'seq'=4,'head'=2] {'seq'}, dimensions={0}, use_global_device_ids=true | all-gather | bytes 640 | tf_op jit(solution)/shard_map/all_gather | solution.py:257
  138.2 5.2 broadcast_in_dim.28
  143.5 8.7 %copy.82 = f32[2,1024,1024]{2,1,0:T(8,128)} copy(f32[2,1024,1024]{1,2,0:T(8,128)} %bitcast.130) | data formatting | bytes 16777216 | tf_op jit(solution)/shard_map/reshape | solution.py:371
  152.2 4.2 fusion.12
  157.6 3.6 fusion.42.enter_ref
  164.5 24.3 %recurrence_forward.1 = (f32[2,1024,1024]{2,1,0:T(8,128)}, bf16[2,8,1024,128]{3,2,1,0:T(8,128)(2,1)S(1)}) custom-call(f32[2,1024,1024]{2,1,0:T(8,128)} %get-tuple-element.80.x_ref, f32[2,1024,16]{2,1,0:T(8,128)S(1)} %get-tuple-element.79.st_ref, f32[2,1024,16]{2,1,0:T(8,128)S(1)} %copy-done.2, f32[2,16,1024]{2,1,0:T(8,128)S(1)} %get-tuple-element.87.cumt_ref, ...), custom_call_target="tpu_custom_call" | custom-call | flops 20000000000 | bytes 30000000 | tf_op jit(solution)/shard_map/recurrence_forward/pallas_call | solution.py:181
  188.8 12.9 %multiply_reduce_fusion.7 = (f32[2048]{0:T(1024)S(1)}, f32[2048,1024]{1,0:T(8,128)}, f32[2048,1024]{1,0:T(8,128)}) fusion(f32[2,1024,1024]{2,1,0:T(8,128)} %get-tuple-element.26.core_ref, bf16[2048,1024]{1,0:T(8,128)(2,1)S(1)} %copy-done.20, bf16[1024,1024]{1,0:T(8,128)(2,1)S(1)} %copy-done), kind=kOutput, calls=%fused_computation.36 | convolution fusion | flops 4309645312 | bytes 31465472 | tf_op jit(solution)/shard_map/dot_general | solution.py:19
  205.5 10.8 %convolution_convert_fusion = bf16[1024,1024]{1,0:T(8,128)(2,1)} fusion(bf16[2048,1024]{1,0:T(8,128)(2,1)} %bitcast.171, f32[2048,1024]{1,0:T(8,128)} %get-tuple-element.68, f32[1024]{0:T(1024)S(1)} %copy-done.54, f32[2048]{0:T(1024)S(1)} %add_rsqrt_fusion), kind=kOutput, calls=%fused_computation.61 | convolution fusion | flops 4302307328 | bytes 14692352 | tf_op jit(solution)/shard_map/dot_general | solution.py:19
  216.5 15.3 %multiply_reduce_fusion = (f32[1024]{0:T(1024)}, f32[2048]{0:T(1024)}, f32[2048,1024]{1,0:T(8,128)}) fusion(f32[2048,1024]{1,0:T(8,128)} %get-tuple-element.68, f32[2048]{0:T(1024)S(1)} %add_rsqrt_fusion, f32[1024]{0:T(1024)S(1)} %copy-done.54, bf16[2048,1024]{1,0:T(8,128)(2,1)} %bitcast.172, bf16[1024,1024]{1,0:T(8,128)(2,1)} %param.31), kind=kOutput, calls=%fused_computation.24 | convolution fusion | flops 4307547136 | bytes 23093248 | tf_op jit(solution)/shard_map/dot_general | solution.py:19
  235.7 16.3 %multiply_reduce_fusion.1 = (f32[1024]{0:T(1024)}, f32[2048,1024]{1,0:T(8,128)}) fusion(f32[2,1024,1024]{2,1,0:T(8,128)} %get-tuple-element.81, f32[2048,1024]{1,0:T(8,128)} %get-tuple-element.106, f32[2048]{0:T(1024)S(1)} %broadcast_multiply_fusion.2, f32[2048,1024]{1,0:T(8,128)} %get-tuple-element.68, f32[2048,1024]{1,0:T(8,128)} %get-tuple-element.107, ...), kind=kLoop, calls=%fused_computation.25 | loop fusion | flops 33553408 | bytes 41967616 | tf_op jit(solution)/shard_map/reduce_sum | solution.py:400
  254.7 7.8 %fusion.67 = f32[2048,1024]{1,0:T(8,128)S(1)} fusion(bf16[1024,1024]{1,0:T(8,128)(2,1)} %param.31, f32[2048,1024]{1,0:T(8,128)} %get-tuple-element.68, f32[1024]{0:T(1024)S(1)} %copy-done.54, f32[2048]{0:T(1024)S(1)} %add_rsqrt_fusion), kind=kOutput, calls=%fused_computation.177 | convolution fusion | flops 4301258752 | bytes 18886656 | tf_op jit(solution)/shard_map/dot_general | solution.py:19
  262.5 3.2 copy-done.16
  267.5 8.5 %fusion.22 = bf16[2,1024,128]{2,1,0:T(8,128)(2,1)} fusion(f32[2,1024,1024]{2,1,0:T(8,128)} %bitcast.131, f32[2,1024,1024]{2,1,0:T(8,128)} %copy.82, bf16[2,1024,256]{2,1,0:T(8,128)(2,1)S(1)} %copy-done.28), kind=kOutput, calls=%fused_computation.68 | convolution fusion | flops 541327360 | bytes 17825792 | tf_op jit(solution)/shard_map/glp,gln->gpn/dot_general | solution.py:402
  276.4 12.7 %fusion.14 = bf16[2048,1024]{1,0:T(8,128)(2,1)S(1)} fusion(f32[2,1024,1024]{2,1,0:T(8,128)} %get-tuple-element.26.core_ref, f32[2048,1024]{1,0:T(8,128)} %get-tuple-element.106, f32[2048]{0:T(1024)} %copy-done.37, f32[2048,1024]{1,0:T(8,128)} %get-tuple-element.68, f32[2048,1024]{1,0:T(8,128)} %get-tuple-element.107, f32[1024]{0:T(1024)S(1)} %copy-done.54, ...), kind=kLoop, calls=%fused_computation.23 | loop fusion | flops 31457280 | bytes 37769216 | tf_op jit(solution)/shard_map/convert_element_type | solution.py:398
  289.1 6.9 fusion.73
  296.0 5.8 convolution_convert_fusion.1
  301.8 38.9 %all-reduce.7.cloned.1.call-done = bf16[1024,1024]{1,0:T(8,128)(2,1)} async-done(((bf16[1024,1024]{1,0:T(8,128)(2,1)}), bf16[1024,1024]{1,0:T(8,128)(2,1)}) %all-reduce.7.cloned.1.call-update) | async-done | bytes 2097168 | tf_op jit(solution)/shard_map/psum | solution.py:296
  340.7 4.1 convert_element_type.208
  344.8 42.7 %all-gather.18.cloned.1.call-done = bf16[8,1024,128]{2,1,0:T(8,128)(2,1)} async-done(((bf16[2,1024,128]{2,1,0:T(8,128)(2,1)}), bf16[8,1024,128]{2,1,0:T(8,128)(2,1)}) %all-gather.18.cloned.1.call-update) | async-done | bytes 2097168 | tf_op jit(solution)/shard_map/all_gather | solution.py:258
  387.5 3.3 fusion.37.later_ref
  395.1 44.3 %recurrence_backward.1 = (f32[2,1024,1024]{2,1,0:T(8,128)}, f32[2,1024,256]{2,1,0:T(8,128)S(1)}, f32[2,1024,16]{2,1,0:T(8,128)S(1)}, f32[2,1024,16]{2,1,0:T(8,128)S(1)}) custom-call(f32[2,1024,1024]{2,1,0:T(8,128)} %get-tuple-element.80.x_ref, f32[2,1024,1024]{2,1,0:T(8,128)} %bitcast.132, f32[2,1024,1024]{2,1,0:T(8,128)} %get-tuple-element.26.core_ref, ...), custom_call_target="tpu_custom_call" | custom-call | flops 60000002048 | bytes 45000000 | tf_op jit(solution)/shard_map/recurrence_backward/pallas_call | solution.py:215
  439.4 18.5 %multiply_reduce_fusion.5 = (f32[1024]{0:T(1024)S(1)}, f32[1024]{0:T(1024)S(1)}, f32[1024]{0:T(1024)S(1)}, f32[1024]{0:T(1024)S(1)}, f32[1024]{0:T(1024)S(1)}, /*index=5*/f32[2,1024,1024]{2,1,0:T(8,128)S(1)}) fusion(f32[2,1024,1024]{2,1,0:T(8,128)} %fusion.20, f32[2,3,1024]{2,1,0:T(4,128)S(1)} %copy-done.31, f32[2,1024,1024]{2,1,0:T(8,128)} %get-tuple-element.28, ...), kind=kLoop, calls=%fused_computation.29 | loop fusion | flops 41937920 | bytes 33599488 | tf_op jit(solution)/shard_map/reduce_sum | solution.py:428
  461.9 4.5 fusion.75
  466.5 13.3 %fusion.4 = bf16[2,1024,1024]{2,1,0:T(8,128)(2,1)S(1)} fusion(f32[2,3,1024]{2,1,0:T(4,128)S(1)} %collective-permute-done.3, f32[2,1024,1024]{2,1,0:T(8,128)} %copy-done.10, f32[1024]{0:T(1024)S(1)} %bitcast.148, f32[1024]{0:T(1024)S(1)} %bitcast.150, f32[1024]{0:T(1024)S(1)} %bitcast.146, f32[1024]{0:T(1024)S(1)} %bitcast.144), kind=kLoop, calls=%fused_computation.8 | loop fusion | flops 23068672 | bytes 12623872 | tf_op jit(solution)/shard_map/convert_element_type | solution.py:437
  484.1 6.1 bitcast_convert_fusion
  493.0 17.3 %add_add_fusion = f32[2048,1024]{1,0:T(8,128)} fusion(f32[2048,1024]{1,0:T(8,128)} %fusion.75, f32[2048,1024]{1,0:T(8,128)S(1)} %fusion.74, f32[2048,1024]{1,0:T(8,128)} %fusion.73, bf16[2048,1024]{1,0:T(8,128)(2,1)} %bitcast.133, bf16[1024,1024]{1,0:T(8,128)(2,1)} %param.20), kind=kOutput, calls=%fused_computation.30 | convolution fusion | flops 4301258752 | bytes 39845888 | tf_op jit(solution)/shard_map/dot_general | solution.py:19
  510.3 3.9 dynamic-slice_convert_fusion
  514.8 4.5 all-reduce.9.cloned.1.call-done
  519.6 3.7 convert_add_fusion.2
  530.3 4.1 convert_element_type.206
  534.4 3.7 multiply_reduce_fusion.9
  540.6 4.9 subtract_multiply_fusion.1
  545.5 76.8 %all-reduce = (f32[512]{0:T(512)}, f32[4,1024]{1,0:T(4,128)}, f32[4,128]{1,0:T(4,128)}, f32[1024]{0:T(1024)}, f32[128]{0:T(128)}, /*index=5*/f32[16]{0:T(128)}, f32[16]{0:T(128)}, f32[16]{0:T(128)}, f32[1024]{0:T(1024)}) all-reduce(f32[512]{0:T(512)S(1)} %get-tuple-element.42, ...), channel_id=1, replica_groups=mesh['batch'=4,'seq'=4,'head'=2] {'batch','seq'}, use_global_device_ids=true, to_apply=%region_8.9 | all-reduce | flops 7344 | bytes 58752 | tf_op jit(solution)/shard_map/psum | solution.py:461
  622.3 5.7 convert_add_fusion.1
  628.0 22.2 %all-reduce.11.cloned.1.call-done = bf16[1024,1024]{1,0:T(8,128)(2,1)} async-done(((bf16[1024,1024]{1,0:T(8,128)(2,1)}), bf16[1024,1024]{1,0:T(8,128)(2,1)}) %all-reduce.11.cloned.1.call-update) | async-done | bytes 2097168 | tf_op jit(solution)/shard_map/psum | solution.py:296
  650.2 4.1 convert_element_type.207
  654.3 111.7 %all-reduce.13.cloned.1.call-done = (f32[1024,128]{1,0:T(8,128)}, f32[1024,16]{0,1:T(8,128)}) async-done(((f32[1024,128]{1,0:T(8,128)}, f32[1024,16]{0,1:T(8,128)}), (f32[1024,128]{1,0:T(8,128)}, f32[1024,16]{0,1:T(8,128)})) %all-reduce.13.cloned.1.call-update) | async-done | bytes 589840 | tf_op jit(solution)/shard_map/psum | solution.py:461
  (257 shorter events, 84.8 us)
Async XLA Ops:
  7.2 181.6 %copy-start = (bf16[1024,1024]{1,0:T(8,128)(2,1)S(1)}, bf16[1024,1024]{1,0:T(8,128)(2,1)}, u32[]{:S(2)}) copy-start(bf16[1024,1024]{1,0:T(8,128)(2,1)} %param.19) | copy-start | bytes 6291460
  7.2 30.8 %copy-start.46 = (bf16[1024,16]{0,1:T(8,128)(2,1)S(1)}, bf16[1024,16]{0,1:T(8,128)(2,1)}, u32[]{:S(2)}) copy-start(bf16[1024,16]{0,1:T(8,128)(2,1)} %param.22) | copy-start | bytes 98308
  7.2 30.8 %copy-start.78 = (f32[16]{0:T(128)S(1)}, f32[16]{0:T(128)}, u32[]{:S(2)}) copy-start(f32[16]{0:T(128)} %param.27) | copy-start | bytes 196
  7.2 18.8 %all-gather.10.cloned.1.call-start = ((), (), s32[]{:S(2)}) async-start(), calls=%async_computation | async-start | bytes 6291456 | tf_op jit(solution)/shard_map/all_gather | solution.py:320
  8.0 89.8 %all-gather.12.cloned.1.call-start = ((), (), s32[]{:S(2)}) async-start(), calls=%async_computation.1 | async-start | bytes 1572864 | tf_op jit(solution)/shard_map/all_gather | solution.py:346
  10.6 141.6 %copy-start.50 = (f32[2,1,512]{2,1,0:T(1,128)}, f32[2,1,512]{2,1,0:T(1,128)S(1)}, u32[]{:S(2)}) copy-start(f32[2,1,512]{2,1,0:T(1,128)S(1)} %convert_element_type.225) | copy-start | bytes 12292
  11.3 28.3 %copy-start.73 = (f32[16]{0:T(128)}, f32[16]{0:T(128)S(1)}, u32[]{:S(2)}) copy-start(f32[16]{0:T(128)S(1)} %exponential_negate_fusion) | copy-start | bytes 196
  12.1 63.2 %copy-start.57 = (f32[128]{0:T(128)}, f32[128]{0:T(128)S(1)}, u32[]{:S(2)}) copy-start(f32[128]{0:T(128)S(1)} %get-tuple-element.100) | copy-start | bytes 1540
  12.1 63.2 %copy-start.59 = (f32[128]{0:T(128)}, f32[128]{0:T(128)S(1)}, u32[]{:S(2)}) copy-start(f32[128]{0:T(128)S(1)} %get-tuple-element.101) | copy-start | bytes 1540
  12.1 63.2 %copy-start.61 = (f32[128]{0:T(128)}, f32[128]{0:T(128)S(1)}, u32[]{:S(2)}) copy-start(f32[128]{0:T(128)S(1)} %get-tuple-element.102) | copy-start | bytes 1540
  12.1 63.2 %copy-start.63 = (f32[128]{0:T(128)}, f32[128]{0:T(128)S(1)}, u32[]{:S(2)}) copy-start(f32[128]{0:T(128)S(1)} %get-tuple-element.103) | copy-start | bytes 1540
  13.0 66.7 %copy-start.38 = (f32[1,1024]{1,0:T(1,128)}, f32[1,1024]{1,0:T(1,128)S(1)}, u32[]{:S(2)}) copy-start(f32[1,1024]{1,0:T(1,128)S(1)} %get-tuple-element.89) | copy-start | bytes 12292
  13.0 66.7 %copy-start.40 = (f32[1,1024]{1,0:T(1,128)}, f32[1,1024]{1,0:T(1,128)S(1)}, u32[]{:S(2)}) copy-start(f32[1,1024]{1,0:T(1,128)S(1)} %get-tuple-element.90) | copy-start | bytes 12292
  13.0 66.7 %copy-start.42 = (f32[1,1024]{1,0:T(1,128)}, f32[1,1024]{1,0:T(1,128)S(1)}, u32[]{:S(2)}) copy-start(f32[1,1024]{1,0:T(1,128)S(1)} %get-tuple-element.91) | copy-start | bytes 12292
  13.1 66.7 %copy-start.44 = (f32[1,1024]{1,0:T(1,128)}, f32[1,1024]{1,0:T(1,128)S(1)}, u32[]{:S(2)}) copy-start(f32[1,1024]{1,0:T(1,128)S(1)} %get-tuple-element.92) | copy-start | bytes 12292
  34.4 40.9 %collective-permute-start.1 = (f32[2,3,128]{2,1,0:T(4,128)S(1)}, f32[2,3,128]{2,1,0:T(4,128)S(1)}, u32[]{:S(2)}, u32[]{:S(2)}) collective-permute-start(f32[2,3,128]{2,1,0:T(4,128)S(1)} %slice.223), channel_id=1, source_target_pairs={{0,2},{2,4},{4,6},{1,3},{3,5},{5,7},{8,10},{10,12},{12,14},{9,11},... | collective-permute-start | bytes 9224 | tf_op jit(solution)/shard_map/ppermute | solution.py:252
  62.0 17.8 %copy-start.65 = (f32[1024]{0:T(1024)S(1)}, f32[1024]{0:T(1024)}, u32[]{:S(2)}) copy-start(f32[1024]{0:T(1024)} %param.25) | copy-start | bytes 12292
  71.5 8.1 %collective-permute-start = (f32[2,3,1024]{2,1,0:T(4,128)S(1)}, f32[2,3,1024]{2,1,0:T(4,128)S(1)}, u32[]{:S(2)}, u32[]{:S(2)}) collective-permute-start(f32[2,3,1024]{2,1,0:T(4,128)S(1)} %slice.218), channel_id=1, source_target_pairs={{0,2},{2,4},{4,6},{1,3},{3,5},{5,7},{8,10},{10,12},{12,14},{9,11},... | collective-permute-start | bytes 73736 | tf_op jit(solution)/shard_map/ppermute | solution.py:252
  75.3 22.5 %copy-start.52 = (f32[2,3,128]{2,1,0:T(4,128)}, f32[2,3,128]{2,1,0:T(4,128)S(1)}, u32[]{:S(2)}) copy-start(f32[2,3,128]{2,1,0:T(4,128)S(1)} %collective-permute-done.1) | copy-start | bytes 9220
  79.6 78.0 %all-gather.16.cloned.1.call-start = ((), (), s32[]{:S(2)}) async-start(), calls=%async_computation.6 | async-start | bytes 2621440 | tf_op jit(solution)/shard_map/all_gather | solution.py:258
  79.7 18.1 %copy-start.30 = (f32[2,3,1024]{2,1,0:T(4,128)}, f32[2,3,1024]{2,1,0:T(4,128)S(1)}, u32[]{:S(2)}) copy-start(f32[2,3,1024]{2,1,0:T(4,128)S(1)} %collective-permute-done) | copy-start | bytes 73732
  107.4 98.1 %all-gather.14.cloned.1.call-start = ((), (), s32[]{:S(2)}) async-start(), calls=%async_computation.2 | async-start | bytes 6291456 | tf_op jit(solution)/shard_map/all_gather | solution.py:323
  108.0 232.7 %all-reduce.7.cloned.1.call-start = ((), (), s32[]{:S(2)}) async-start(), calls=%async_computation.3 | async-start | bytes 4194304 | tf_op jit(solution)/shard_map/psum | solution.py:296
  120.4 31.8 %copy-start.32 = (f32[1,8,2,128]{3,1,2,0:T(8,128)}, f32[1,8,2,128]{3,1,2,0:T(8,128)S(1)}, u32[]{:S(2)}) copy-start(f32[1,8,2,128]{3,1,2,0:T(8,128)S(1)} %copy.102) | copy-start | bytes 24580
  164.5 24.3 %copy-start.20 = (bf16[2048,1024]{1,0:T(8,128)(2,1)S(1)}, bf16[2048,1024]{1,0:T(8,128)(2,1)}, u32[]{:S(2)}) copy-start(bf16[2048,1024]{1,0:T(8,128)(2,1)} %fusion.12) | copy-start | bytes 12582916
  188.8 16.7 %copy-start.54 = (f32[1024]{0:T(1024)S(1)}, f32[1024]{0:T(1024)}, u32[]{:S(2)}) copy-start(f32[1024]{0:T(1024)} %param.30) | copy-start | bytes 12292
  216.3 171.3 %all-gather.18.cloned.1.call-start = ((), (), s32[]{:S(2)}) async-start(), calls=%async_computation.7 | async-start | bytes 2621440 | tf_op jit(solution)/shard_map/all_gather | solution.py:258
  267.4 252.2 %collective-permute-start.2 = (bf16[2048,512]{1,0:T(8,128)(2,1)}, bf16[2048,512]{1,0:T(8,128)(2,1)}, u32[]{:S(2)}, u32[]{:S(2)}) collective-permute-start(bf16[2048,512]{1,0:T(8,128)(2,1)} %dynamic-slice_convert_fusion.1), channel_id=1, source_target_pairs={{0,1},{1,0},{2,3},{3,2},{4,5},{5,4},{6,7},{7,6},{8,9},{9,8},{10,11... | collective-permute-start | bytes 6291464 | tf_op jit(solution)/shard_map/ppermute | solution.py:274
  276.0 243.3 %all-reduce.9.cloned.1.call-start = ((), (), s32[]{:S(2)}) async-start(), calls=%async_computation.4 | async-start | bytes 4194304 | tf_op jit(solution)/shard_map/psum | solution.py:296
  301.8 85.8 %copy-start.34 = (f32[2,1024]{1,0:T(2,128)S(1)}, f32[2,1024]{1,0:T(2,128)}, u32[]{:S(2)}) copy-start(f32[2,1024]{1,0:T(2,128)} %mul.472) | copy-start | bytes 24580
  301.8 85.8 %copy-start.35 = (f32[2,1024]{1,0:T(2,128)S(1)}, f32[2,1024]{1,0:T(2,128)}, u32[]{:S(2)}) copy-start(f32[2,1024]{1,0:T(2,128)} %mul.469) | copy-start | bytes 24580
  301.8 85.8 %copy-start.36 = (f32[2,1024]{1,0:T(2,128)S(1)}, f32[2,1024]{1,0:T(2,128)}, u32[]{:S(2)}) copy-start(f32[2,1024]{1,0:T(2,128)} %mul.465) | copy-start | bytes 24580
  301.8 85.8 %copy-start.48 = (f32[2,1024]{1,0:T(2,128)S(1)}, f32[2,1024]{1,0:T(2,128)}, u32[]{:S(2)}) copy-start(f32[2,1024]{1,0:T(2,128)} %broadcast_multiply_fusion.3) | copy-start | bytes 24580
  301.8 89.1 %copy-start.3 = (f32[2,1024,16]{2,1,0:T(8,128)S(1)}, f32[2,1024,16]{2,1,0:T(8,128)}, u32[]{:S(2)}) copy-start(f32[2,1024,16]{2,1,0:T(8,128)} %copy.80.cum_ref) | copy-start | bytes 393220
  344.8 305.4 %all-reduce.11.cloned.1.call-start = ((), (), s32[]{:S(2)}) async-start(), calls=%async_computation.5 | async-start | bytes 4194304 | tf_op jit(solution)/shard_map/psum | solution.py:296
  395.1 44.3 %copy-start.31 = (f32[2,3,1024]{2,1,0:T(4,128)S(1)}, f32[2,3,1024]{2,1,0:T(4,128)}, u32[]{:S(2)}) copy-start(f32[2,3,1024]{2,1,0:T(4,128)} %copy-done.30) | copy-start | bytes 73732
  439.4 21.5 %copy-start.24 = (f32[2,1024,16]{2,1,0:T(8,128)S(1)}, f32[2,1024,16]{2,1,0:T(8,128)}, u32[]{:S(2)}) copy-start(f32[2,1024,16]{2,1,0:T(8,128)} %copy-done.23) | copy-start | bytes 393220
  439.4 21.5 %copy-start.74 = (f32[16]{0:T(128)S(1)}, f32[16]{0:T(128)}, u32[]{:S(2)}) copy-start(f32[16]{0:T(128)} %copy-done.73) | copy-start | bytes 196
  439.4 22.5 %copy-start.47 = (bf16[1024,16]{0,1:T(8,128)(2,1)S(1)}, bf16[1024,16]{0,1:T(8,128)(2,1)}, u32[]{:S(2)}) copy-start(bf16[1024,16]{0,1:T(8,128)(2,1)} %param.22) | copy-start | bytes 98308
  458.0 8.5 %collective-permute-start.3 = (f32[2,3,1024]{2,1,0:T(4,128)S(1)}, f32[2,3,1024]{2,1,0:T(4,128)S(1)}, u32[]{:S(2)}, u32[]{:S(2)}) collective-permute-start(f32[2,3,1024]{2,1,0:T(4,128)S(1)} %slice.251), channel_id=1, source_target_pairs={{2,0},{4,2},{6,4},{3,1},{5,3},{7,5},{10,8},{12,10},{14,12},{11,9},... | collective-permute-start | bytes 73736 | tf_op jit(solution)/shard_map/ppermute | solution.py:252
  460.9 19.0 %collective-permute-start.4 = (bf16[2048,128]{1,0:T(8,128)(2,1)}, bf16[2048,128]{1,0:T(8,128)(2,1)}, u32[]{:S(2)}, u32[]{:S(2)}) collective-permute-start(bf16[2048,128]{1,0:T(8,128)(2,1)} %dynamic-slice_convert_fusion.2), channel_id=1, source_target_pairs={{0,1},{1,0},{2,3},{3,2},{4,5},{5,4},{6,7},{7,6},{8,9},{9,8},{10,11... | collective-permute-start | bytes 1572872 | tf_op jit(solution)/shard_map/ppermute | solution.py:274
  466.5 17.7 %copy-start.14 = (bf16[2,1024,1024]{2,1,0:T(8,128)(2,1)S(1)}, bf16[2,1024,1024]{2,1,0:T(8,128)(2,1)}, u32[]{:S(2)}) copy-start(bf16[2,1024,1024]{2,1,0:T(8,128)(2,1)} %all-gather.10.cloned.1.call-done) | copy-start | bytes 12582916
  466.5 17.7 %copy-start.51 = (f32[2,1,512]{2,1,0:T(1,128)S(1)}, f32[2,1,512]{2,1,0:T(1,128)}, u32[]{:S(2)}) copy-start(f32[2,1,512]{2,1,0:T(1,128)} %copy-done.50) | copy-start | bytes 12292
  466.5 17.7 %copy-start.56 = (f32[2,1024]{1,0:T(2,128)S(1)}, f32[2,1024]{1,0:T(2,128)}, u32[]{:S(2)}) copy-start(f32[2,1024]{1,0:T(2,128)} %copy-done.55) | copy-start | bytes 24580
  482.8 7.5 collective-permute-start.5
  514.3 20.1 %collective-permute-start.6 = (bf16[2048,512]{1,0:T(8,128)(2,1)}, bf16[2048,512]{1,0:T(8,128)(2,1)}, u32[]{:S(2)}, u32[]{:S(2)}) collective-permute-start(bf16[2048,512]{1,0:T(8,128)(2,1)} %dynamic-slice_convert_fusion), channel_id=1, source_target_pairs={{0,1},{1,0},{2,3},{3,2},{4,5},{5,4},{6,7},{7,6},{8,9},{9,8},{10,11... | collective-permute-start | bytes 6291464 | tf_op jit(solution)/shard_map/ppermute | solution.py:274
  519.3 246.7 %all-reduce.13.cloned.1.call-start = ((), (), s32[]{:S(2)}) async-start(), calls=%async_computation.8 | async-start | bytes 1179648 | tf_op jit(solution)/shard_map/psum | solution.py:461
  622.3 147.1 %copy-start.1 = (bf16[1024,1024]{1,0:T(8,128)(2,1)S(1)}, bf16[1024,1024]{1,0:T(8,128)(2,1)}, u32[]{:S(2)}) copy-start(bf16[1024,1024]{1,0:T(8,128)(2,1)} %param.19) | copy-start | bytes 6291460
  (48 other events, 347.4 us)
Sparse Core Ops, SparseCore 0:
  9.6 16.3 all-gather.9
  79.7 8.0 all-gather.11
  107.5 45.0 all-gather.15
  154.0 12.3 all-gather.13
  216.4 124.2 all-reduce.6
  342.2 45.2 all-gather.17
  394.5 124.7 all-reduce.8
  524.7 125.4 all-reduce.10
  657.0 108.9 all-reduce.12
